TPU v7x, 512 devices: a whole 4x4x16 slice. The times are simulated.
512 devices in a mesh: layer: 16 (over z_lo, y), ex: 32 (over x, z_hi, core).
Axes of the slice: x: 4, y: 4, z: 16 (z_hi: 4, z_lo: 4; z = z_hi * 4 + z_lo), core: 2. Of those that a mesh axis runs over, the one named last changes fastest.
Arguments:
- train_grads: bfloat16 [16, 16384, 2048], P('layer', 'ex'), may hold values from -0.03125 to 0.03125
- query_grads: bfloat16 [16, 1024, 2048], P('layer', 'ex'), may hold values from -6 to 6
- inverse_fisher: bfloat16 [16, 2048, 2048], P('layer', 'ex'), may hold values from -1 to 6, as said below
Outputs:
- scores: float32 [16384, 1024], P('ex', 'layer')
Inputs may be any that keep to these rules, and one draw needn't show every extreme that they name: `inverse_fisher`: each layer's block is exactly symmetric.
All inputs are finite; a program needn't handle non-finite values.
Results may differ from a plain program's by a relative error of at most 0.0029.
Values may be sent and summed in bfloat16 or wider, within the bound.
No kernel may reach another device: no remote copies, remote signals or barrier semaphores. Data moves between devices by JAX's collectives and lax.ppermute only.
A program may use at most 64 MiB of HBM per device.

v0:
```python
import jax
import jax.numpy as jnp
from jax import lax
from jax.sharding import PartitionSpec as P


def on_device(train_grads, query_grads, inverse_fisher):
    train_rows = train_grads[0]
    query_rows = query_grads[0]
    fisher_rows = inverse_fisher[0]
    conditioned = jnp.dot(
        query_rows,
        lax.all_gather(fisher_rows, "ex", axis=0, tiled=True),
        preferred_element_type=jnp.float32,
    ).astype(jnp.bfloat16)
    partial_value = lax.dot_general(
        train_rows,
        lax.all_gather(conditioned, "ex", axis=0, tiled=True),
        (((1,), (1,)), ((), ())),
        preferred_element_type=jnp.float32,
    )
    return lax.psum_scatter(partial_value, "layer", scatter_dimension=1, tiled=True)


def solution(mesh):
    return jax.shard_map(
        on_device,
        mesh=mesh,
        in_specs=(P("layer", "ex", None), P("layer", "ex", None), P("layer", "ex", None)),
        out_specs=P("ex", "layer"),
        check_vma=False,
    )
```

profile of v0, /device:TPU:4, one launch (start us, length us, event | category | flops | bytes accessed | tf_op | source)
XLA Modules:
  0.0 348.5 jit_solution(13845109691409250169)
XLA Ops:
  6.5 0.0 copy-start
  6.5 0.0 all-gather.6.cloned.1.call-start
  6.5 0.7 all-gather.6.cloned.1.call-update
  7.3 0.0 all-gather.4.cloned.1.call-start
  7.3 143.0 %all-gather.6.cloned.1.call-done = bf16[1,2048,2048]{2,1,0:T(8,128)(2,1)} async-done(((bf16[1,64,2048]{2,1,0:T(8,128)(2,1)}), bf16[1,2048,2048]{2,1,0:T(8,128)(2,1)}) %all-gather.6.cloned.1.call-update) | async-done | bytes 8388624 | tf_op jit(solution)/shard_map/all_gather | solution.py:13
  150.4 5.7 %fusion.2 = bf16[32,2048]{1,0:T(8,128)(2,1)} fusion(bf16[1,2048,2048]{2,1,0:T(8,128)(2,1)} %all-gather.6.cloned.1.call-done, bf16[1,32,2048]{2,1,0:T(8,128)(2,1)} %param.4), kind=kOutput, calls=%fused_computation.2 | convolution fusion | flops 268500992 | bytes 8650752 | tf_op jit(solution)/shard_map/dot_general | solution.py:11
  156.0 0.0 all-gather.4.cloned.1.call-update
  156.0 0.0 reduce-scatter.2.cloned.1.call-start
  156.1 90.8 %all-gather.4.cloned.1.call-done = bf16[1024,2048]{1,0:T(8,128)(2,1)} async-done(((bf16[32,2048]{1,0:T(8,128)(2,1)}), bf16[1024,2048]{1,0:T(8,128)(2,1)}) %all-gather.4.cloned.1.call-update) | async-done | bytes 4194320 | tf_op jit(solution)/shard_map/all_gather | solution.py:18
  246.9 0.0 copy-done
  246.9 5.9 %fusion.7 = f32[512,1024]{0,1:T(8,128)} fusion(bf16[1024,2048]{1,0:T(8,128)(2,1)} %all-gather.4.cloned.1.call-done, bf16[1,512,2048]{2,1,0:T(8,128)(2,1)S(1)} %copy-done), kind=kOutput, calls=%fused_computation.5 | convolution fusion | flops 2147483648 | bytes 8388608 | tf_op jit(solution)/shard_map/dot_general | solution.py:16
  252.8 0.0 reduce-scatter.2.cloned.1.call-update
  252.8 89.2 %reduce-scatter.2.cloned.1.call-done = f32[512,64]{0,1:T(8,128)} async-done(((f32[512,1024]{0,1:T(8,128)}), f32[512,64]{0,1:T(8,128)}) %reduce-scatter.2.cloned.1.call-update) | async-done | bytes 131088 | tf_op jit(solution)/shard_map/reduce_scatter | solution.py:22
Async XLA Ops:
  6.5 240.4 %copy-start = (bf16[1,512,2048]{2,1,0:T(8,128)(2,1)S(1)}, bf16[1,512,2048]{2,1,0:T(8,128)(2,1)}, u32[]{:S(2)}) copy-start(bf16[1,512,2048]{2,1,0:T(8,128)(2,1)} %param.3) | copy-start | bytes 6291460
  6.5 143.8 %all-gather.6.cloned.1.call-start = ((), (), s32[]{:S(2)}) async-start(), calls=%async_computation.3 | async-start | bytes 8650752 | tf_op jit(solution)/shard_map/all_gather | solution.py:13
  7.3 239.7 %all-gather.4.cloned.1.call-start = ((), (), s32[]{:S(2)}) async-start(), calls=%async_computation.1 | async-start | bytes 4325376 | tf_op jit(solution)/shard_map/all_gather | solution.py:18
  156.0 185.9 %reduce-scatter.2.cloned.1.call-start = ((), (), s32[]{:S(2)}) async-start(), calls=%async_computation.2 | async-start | bytes 2228224 | tf_op jit(solution)/shard_map/reduce_scatter | solution.py:22
Sparse Core Ops, SparseCore 0:
  10.5 139.8 all-gather.5
  156.2 90.7 all-gather.3
  252.9 88.9 reduce-scatter.1
where the time goes:
time: 349 us
  waiting for transfers between devices  324 us (93%)
  between operations  13.1 us (4%)
  matrix products  11.5 us (3%)
    all_gather x1, waiting for transfers between devices, on_device(): lax.all_gather(fisher_rows, 'ex', axis=0, tiled=True)  143 us
    all_gather x1, waiting for transfers between devices, on_device(): lax.all_gather(conditioned, 'ex', axis=0, tiled=True)  90.8 us
    reduce_scatter x1, waiting for transfers between devices, on_device(): lax.psum_scatter(partial_value, 'layer', scatter_dimension=1, tiled=True)  89.2 us
  transfers between devices with their start and end apart: 3, of which 3 were waited for; matrix products, arithmetic and copies ran while one was open for 0% of the time, Pallas kernels for 0%

commit v1 on v0

v1 whole, which is shorter than its diff:
```python
import jax
import jax.numpy as jnp
from jax import lax
from jax.sharding import Mesh
from jax.sharding import PartitionSpec as P

LAYER = ("zl", "y")
EX = ("x", "zh", "c")


def copies(block, n):
    return jnp.broadcast_to(block[None], (n,) + block.shape)


def on_device(train_grads, query_grads, inverse_fisher):
    train, query, fisher = train_grads[0], query_grads[0], inverse_fisher[0]
    rows, k = train.shape
    plane = lax.all_to_all(copies(fisher, 8), ("x", "c"), 0, 0)
    plane = plane.reshape(-1, k)
    ordered = train.reshape(rows, 4, 4, k // 16).swapaxes(1, 2).reshape(rows, k)
    pair = lax.all_gather(ordered, "c", axis=0, tiled=True)
    queries = lax.all_gather(query, "zh", axis=0, tiled=True)
    conditioned = lax.dot_general(
        queries, plane, (((1,), (1,)), ((), ())), preferred_element_type=jnp.float32
    ).astype(jnp.bfloat16)
    conditioned = lax.all_gather(conditioned, "zh", axis=1, tiled=True)
    conditioned = lax.all_to_all(copies(conditioned, 4), "x", 0, 0).reshape(-1, k)
    part = lax.dot_general(
        conditioned, pair, (((1,), (1,)), ((), ())), preferred_element_type=jnp.float32
    ).astype(jnp.bfloat16)
    part = part.reshape(16, -1, 2, rows).swapaxes(1, 2).reshape(32, -1, rows)
    part = lax.all_to_all(part, LAYER + ("c",), 0, 0)
    total = part.reshape(16, -1, rows).astype(jnp.float32).sum(axis=0)
    return total.T


def solution(mesh):
    split = Mesh(mesh.devices.reshape(4, 4, 4, 4, 2), LAYER + EX)
    spec = P(LAYER, EX, None)
    return jax.shard_map(
        on_device,
        mesh=split,
        in_specs=(spec, spec, spec),
        out_specs=P(EX, LAYER),
        check_vma=False,
    )
```

time: 349 us -> 153 us (0.44)
  the two profiles are of different devices: /device:TPU:4 before, /device:TPU:1 now
where the time goes in v1:
time: 153 us; the launch traced here: 152 us
  blocking collectives  114 us (75%)
  between operations  13.4 us (9%)
  starting transfers between devices  10.5 us (7%)
  local copies, waits for them, and re-layouts  8.17 us (5%)
  matrix products  5.34 us (3%)
    all_to_all x1, blocking collectives, on_device(): part = lax.all_to_all(part, LAYER + ('c',), 0, 0)  36.9 us
    all_gather x1, blocking collectives, on_device(): queries = lax.all_gather(query, 'zh', axis=0, tiled=True)  26.2 us
    all_gather x1, blocking collectives, on_device(): conditioned = lax.all_gather(conditioned, 'zh', axis=1, tiled=True)  25.8 us
    all_to_all x1, blocking collectives, on_device(): lax.all_to_all(copies(conditioned, 4), 'x', 0, 0).reshape(-1, k)  25 us
    all_to_all x1, starting transfers between devices, on_device(): plane = lax.all_to_all(copies(fisher, 8), ('x', 'c'), 0, 0)  10.5 us
    dot_general x1, matrix products, on_device(): lax.dot_general(conditioned, pair, (((1,), (1,)), ((), ())), preferred_el...  4.51 us
    unnamed x5, local copies, waits for them, and re-layouts  3.79 us
  transfers between devices with their start and end apart: 2, of which 1 were waited for; matrix products, arithmetic and copies ran while one was open for 2% of the time, Pallas kernels for 0%

profile of v1, /device:TPU:1, one launch (start us, length us, event | category | flops | bytes accessed | tf_op | source)
XLA Modules:
  0.0 152.4 jit_solution(4712361635056827494)
XLA Ops:
  6.5 0.0 all-gather.3.cloned.1.call-start
  6.5 2.9 %copy.5 = bf16[1,512,2048]{1,2,0:T(8,128)(2,1)S(1)} copy(bf16[1,512,2048]{2,1,0:T(8,128)(2,1)} %param.3) | data formatting | bytes 4194304 | tf_op args[0]
  9.4 1.5 %copy.6 = bf16[512,4,4,128]{0,3,2,1:T(8,128)(2,1)} copy(bf16[512,4,4,128]{0,3,1,2:T(8,128)(2,1)S(1)} %bitcast.23) | data formatting | bytes 4194304 | tf_op jit(solution)/shard_map/transpose | solution.py:20
  10.9 0.0 copy-start
  10.9 0.0 all-gather.3.cloned.1.call-update
  11.0 0.9 copy-done
  11.9 1.6 %broadcast_in_dim.14 = bf16[8,64,2048]{2,1,0:T(8,128)(2,1)} broadcast(bf16[64,2048]{1,0:T(8,128)(2,1)S(1)} %bitcast.27), dimensions={1,2} | broadcast | bytes 2359296 | tf_op jit(solution)/shard_map/broadcast_in_dim | solution.py:12
  13.5 0.0 copy-start.1
  13.5 10.5 %all-to-all-start = ((bf16[8,64,2048]{2,1,0:T(8,128)(2,1)}), bf16[8,64,2048]{2,1,0:T(8,128)(2,1)S(1)}, u32[]{:S(2)}, u32[]{:S(2)}) async-start(bf16[8,64,2048]{2,1,0:T(8,128)(2,1)} %broadcast_in_dim.14), calls=%async_computation | async-start | bytes 4194304 | tf_op jit(solution)/shard_map/all_to_all | solution.py:18
  24.0 0.0 copy-done.1
  24.0 26.2 %all-gather = bf16[1,128,2048]{2,1,0:T(8,128)(2,1)S(1)} all-gather(bf16[1,32,2048]{2,1,0:T(8,128)(2,1)S(1)} %copy-done.1), channel_id=2, replica_groups=mesh['zl'=4,'y'=4,'x'=4,'zh'=4,'c'=2] {'zh'}, dimensions={1}, use_global_device_ids=true | all-gather | bytes 655360 | tf_op jit(solution)/shard_map/all_gather | solution.py:22
  50.2 0.2 all-to-all-done
  50.4 0.8 convolution_convert_fusion.1
  51.2 25.8 %all_gather.10 = bf16[128,2048]{1,0:T(8,128)(2,1)S(1)} all-gather(bf16[128,512]{1,0:T(8,128)(2,1)S(1)} %convolution_convert_fusion.1), channel_id=1, replica_groups=mesh['zl'=4,'y'=4,'x'=4,'zh'=4,'c'=2] {'zh'}, dimensions={1}, use_global_device_ids=true | all-gather | bytes 655360 | tf_op jit(solution)/shard_map/all_gather | solution.py:26
  77.0 0.2 broadcast_in_dim.15
  77.3 25.0 %all_to_all.15 = bf16[4,128,2048]{2,1,0:T(8,128)(2,1)S(1)} all-to-all(bf16[4,128,2048]{2,1,0:T(8,128)(2,1)S(1)} %broadcast_in_dim.15), channel_id=1, replica_groups=mesh['zl'=4,'y'=4,'x'=4,'zh'=4,'c'=2] {'x'}, dimensions={0} | all-to-all | bytes 4194304 | tf_op jit(solution)/shard_map/all_to_all | solution.py:27
  102.3 0.0 all-gather.3.cloned.1.call-done
  102.3 4.5 %convolution_convert_fusion = bf16[512,1024]{1,0:T(8,128)(2,1)S(1)} fusion(bf16[512,2048]{1,0:T(8,128)(2,1)S(1)} %bitcast.26, bf16[1024,2048]{0,1:T(8,128)(2,1)} %all-gather.3.cloned.1.call-done), kind=kOutput, calls=%fused_computation.1 | convolution fusion | flops 2148007936 | bytes 7340032 | tf_op jit(solution)/shard_map/dot_general | solution.py:28
  106.8 0.8 reshape.22
  107.6 0.2 copy.7
  107.8 36.9 %all_to_all.16 = bf16[32,32,512]{2,1,0:T(8,128)(2,1)S(1)} all-to-all(bf16[32,32,512]{2,1,0:T(8,128)(2,1)S(1)} %bitcast.24), channel_id=1, replica_groups=mesh['zl'=4,'y'=4,'x'=4,'zh'=4,'c'=2] {'zl','y','c'}, dimensions={0} | all-to-all | bytes 2097152 | tf_op jit(solution)/shard_map/all_to_all | solution.py:32
  144.8 0.8 convert_reduce_fusion
Async XLA Ops:
  6.5 95.7 %all-gather.3.cloned.1.call-start = ((), (), s32[]{:S(2)}) async-start(), calls=%async_computation.3 | async-start | bytes 6291456 | tf_op jit(solution)/shard_map/all_gather | solution.py:21
  10.9 0.9 copy-start
  13.5 10.5 %copy-start.1 = (bf16[1,32,2048]{2,1,0:T(8,128)(2,1)S(1)}, bf16[1,32,2048]{2,1,0:T(8,128)(2,1)}, u32[]{:S(2)}) copy-start(bf16[1,32,2048]{2,1,0:T(8,128)(2,1)} %param.4) | copy-start | bytes 393220
  13.5 36.9 %all-to-all-start = ((bf16[8,64,2048]{2,1,0:T(8,128)(2,1)}), bf16[8,64,2048]{2,1,0:T(8,128)(2,1)S(1)}, u32[]{:S(2)}, u32[]{:S(2)}) async-start(bf16[8,64,2048]{2,1,0:T(8,128)(2,1)} %broadcast_in_dim.14), calls=%async_computation | async-start | bytes 4194304 | tf_op jit(solution)/shard_map/all_to_all | solution.py:18
Sparse Core Ops, SparseCore 0:
  11.1 30.8 all-gather.2

commit v2 on v1

v2 whole, which is shorter than its diff:
```python
import jax
import jax.numpy as jnp
from jax import lax
from jax.sharding import Mesh
from jax.sharding import PartitionSpec as P

LAYER = ("zl", "y")
EX = ("x", "zh", "c")
SWAP = [(0, 1), (1, 0)]


def copies(block, n):
    return jnp.broadcast_to(block[None], (n,) + block.shape)


def rows_by_rows(a, b):
    return lax.dot_general(
        a, b, (((1,), (1,)), ((), ())), preferred_element_type=jnp.float32
    ).astype(jnp.bfloat16)


def on_device(train_grads, query_grads, inverse_fisher):
    train, query, fisher = train_grads[0], query_grads[0], inverse_fisher[0]
    rows, k = train.shape
    plane = lax.all_to_all(copies(fisher, 8), ("x", "c"), 0, 0)
    plane = plane.reshape(-1, k)
    other = lax.ppermute(train, "c", SWAP)
    queries = lax.all_gather(query, "zh", axis=0, tiled=True)
    conditioned = rows_by_rows(queries, plane)
    conditioned = lax.all_gather(conditioned, "zh", axis=0)
    conditioned = conditioned.reshape(4, -1, 4, k // 16).transpose(1, 2, 0, 3)
    conditioned = conditioned.reshape(-1, k)
    conditioned = lax.all_to_all(copies(conditioned, 4), "x", 0, 0).reshape(-1, k)
    own, far = rows_by_rows(conditioned, train), rows_by_rows(conditioned, other)
    own, far = own.reshape(16, -1, rows), far.reshape(16, -1, rows)
    first = lax.axis_index("c") == 0
    part = jnp.stack([jnp.where(first, own, far), jnp.where(first, far, own)], axis=1)
    part = lax.all_to_all(part.reshape(32, -1, rows), LAYER + ("c",), 0, 0)
    total = part.reshape(16, -1, rows).astype(jnp.float32).sum(axis=0)
    return total.T


def solution(mesh):
    split = Mesh(mesh.devices.reshape(4, 4, 4, 4, 2), LAYER + EX)
    spec = P(LAYER, EX, None)
    return jax.shard_map(
        on_device,
        mesh=split,
        in_specs=(spec, spec, spec),
        out_specs=P(EX, LAYER),
        check_vma=False,
    )
```

time: 153 us -> 139 us (0.908)
  blocking collectives: 114 us -> 87.4 us
  waiting for transfers between devices: 0.17 us -> 22.7 us
  between operations: 13.4 us -> 0.09 us
  starting transfers between devices: 10.5 us -> 16.1 us
  local copies, waits for them, and re-layouts: 8.17 us -> 4.82 us
    all_to_all x2 -> x1, blocking collectives: 62 us -> 35.6 us  [on_device(): part = lax.all_to_all(part.reshape(32, -1, rows), LAYER + ('c',), 0, 0)]
    all_to_all x0 -> x1, waiting for transfers between devices: none -> 22.7 us  [on_device(): lax.all_to_all(copies(conditioned, 4), 'x', 0, 0).reshape(-1, k)]
    unnamed x5 -> x2, local copies, waits for them, and re-layouts: 3.79 us -> 0.01 us
    all_to_all x0 -> x1, starting transfers between devices: none -> 3.61 us  [on_device(): lax.all_to_all(copies(conditioned, 4), 'x', 0, 0).reshape(-1, k)]
    broadcast_in_dim x2 -> x3, local copies, waits for them, and re-layouts: 1.84 us -> 4.31 us  [copies(): return jnp.broadcast_to(block[None], (n,) + block.shape)]
    ppermute x0 -> x1, starting transfers between devices: none -> 2.02 us  [on_device(): other = lax.ppermute(train, 'c', SWAP)]
    transpose x1 -> x0, local copies, waits for them, and re-layouts: 1.53 us -> none  [on_device(): ordered = train.reshape(rows, 4, 4, k // 16).swapaxes(1, 2).reshape(rows, k)]
    dot_general x2 -> x3, matrix products: 5.34 us -> 6.58 us  [rows_by_rows(): lax.dot_general(a, b, (((1,), (1,)), ((), ())), preferred_element_type=jn...]
  transfers between devices with their start and end apart: 2 -> 3, of which waited for: 1 -> 1; matrix products, arithmetic and copies ran while one was open for 2% -> 4% of each run, Pallas kernels for 0% -> 0%
where the time goes in v2:
time: 139 us
  blocking collectives  87.4 us (63%)
  waiting for transfers between devices  22.7 us (16%)
  starting transfers between devices  16.1 us (12%)
  matrix products  6.58 us (5%)
  local copies, waits for them, and re-layouts  4.82 us (3%)
    all_to_all x1, blocking collectives, on_device(): part = lax.all_to_all(part.reshape(32, -1, rows), LAYER + ('c',), 0, 0)  35.6 us
    all_gather x1, blocking collectives, on_device(): queries = lax.all_gather(query, 'zh', axis=0, tiled=True)  26.5 us
    all_gather x1, blocking collectives, on_device(): conditioned = lax.all_gather(conditioned, 'zh', axis=0)  25.3 us
    all_to_all x1, waiting for transfers between devices, on_device(): lax.all_to_all(copies(conditioned, 4), 'x', 0, 0).reshape(-1, k)  22.7 us
    all_to_all x1, starting transfers between devices, on_device(): plane = lax.all_to_all(copies(fisher, 8), ('x', 'c'), 0, 0)  10.5 us
    dot_general x3, matrix products, rows_by_rows(): lax.dot_general(a, b, (((1,), (1,)), ((), ())), preferred_element_type=jn...  6.58 us
    broadcast_in_dim x3, local copies, waits for them, and re-layouts, copies(): return jnp.broadcast_to(block[None], (n,) + block.shape)  4.31 us
    all_to_all x1, starting transfers between devices, on_device(): lax.all_to_all(copies(conditioned, 4), 'x', 0, 0).reshape(-1, k)  3.61 us
  transfers between devices with their start and end apart: 3, of which 1 were waited for; matrix products, arithmetic and copies ran while one was open for 4% of the time, Pallas kernels for 0%

profile of v2, /device:TPU:1, one launch (start us, length us, event | category | flops | bytes accessed | tf_op | source)
XLA Modules:
  0.0 138.6 jit_solution(10318437755645606602)
XLA Ops:
  0.0 2.5 %broadcast_in_dim.15 = bf16[8,64,2048]{2,1,0:T(8,128)(2,1)} broadcast(bf16[64,2048]{1,0:T(8,128)(2,1)} %bitcast.36), dimensions={1,2} | broadcast | bytes 2359296 | tf_op jit(solution)/shard_map/broadcast_in_dim | solution.py:13
  2.5 0.0 copy-start
  2.5 10.5 %all-to-all-start = ((bf16[8,64,2048]{2,1,0:T(8,128)(2,1)}), bf16[8,64,2048]{2,1,0:T(8,128)(2,1)S(1)}, u32[]{:S(2)}, u32[]{:S(2)}) async-start(bf16[8,64,2048]{2,1,0:T(8,128)(2,1)} %broadcast_in_dim.15), calls=%async_computation | async-start | bytes 4194304 | tf_op jit(solution)/shard_map/all_to_all | solution.py:25
  13.0 2.0 %collective-permute-start = (bf16[512,2048]{1,0:T(8,128)(2,1)}, bf16[512,2048]{1,0:T(8,128)(2,1)}, u32[]{:S(2)}, u32[]{:S(2)}) collective-permute-start(bf16[512,2048]{1,0:T(8,128)(2,1)} %bitcast.37), channel_id=1, source_target_pairs={{0,1},{1,0},{2,3},{3,2},{4,5},{5,4},{6,7},{7,6},{8,9},{9,8},{10,11... | collective-permute-start | bytes 6291464 | tf_op jit(solution)/shard_map/ppermute | solution.py:27
  15.1 0.0 copy-done
  15.1 26.5 %all-gather = bf16[1,128,2048]{2,1,0:T(8,128)(2,1)S(1)} all-gather(bf16[1,32,2048]{2,1,0:T(8,128)(2,1)S(1)} %copy-done), channel_id=2, replica_groups=mesh['zl'=4,'y'=4,'x'=4,'zh'=4,'c'=2] {'zh'}, dimensions={1}, use_global_device_ids=true | all-gather | bytes 655360 | tf_op jit(solution)/shard_map/all_gather | solution.py:28
  41.5 0.0 all-to-all-done
  41.5 0.8 convolution_convert_fusion.2
  42.4 25.3 %all-gather.1 = bf16[512,512]{1,0:T(8,128)(2,1)S(1)} all-gather(bf16[128,512]{1,0:T(8,128)(2,1)S(1)} %convolution_convert_fusion.2), channel_id=3, replica_groups=mesh['zl'=4,'y'=4,'x'=4,'zh'=4,'c'=2] {'zh'}, dimensions={0}, use_global_device_ids=true | all-gather | bytes 655360 | tf_op jit(solution)/shard_map/all_gather | solution.py:30
  67.7 0.1 reshape.57
  67.8 0.4 copy.4
  68.2 0.2 copy.5
  68.4 1.6 %broadcast_in_dim.17 = bf16[4,128,2048]{2,1,0:T(8,128)(2,1)} broadcast(bf16[128,2048]{1,0:T(8,128)(2,1)S(1)} %copy.5), dimensions={1,2} | broadcast | bytes 2621440 | tf_op jit(solution)/shard_map/broadcast_in_dim | solution.py:13
  70.0 3.6 %all-to-all-start.1 = ((bf16[4,128,2048]{2,1,0:T(8,128)(2,1)}), bf16[4,128,2048]{2,1,0:T(8,128)(2,1)S(1)}, u32[]{:S(2)}, u32[]{:S(2)}) async-start(bf16[4,128,2048]{2,1,0:T(8,128)(2,1)} %broadcast_in_dim.17), calls=%async_computation.1 | async-start | bytes 4194304 | tf_op jit(solution)/shard_map/all_to_all | solution.py:33
  73.6 22.7 %all-to-all-done.1 = bf16[4,128,2048]{2,1,0:T(8,128)(2,1)S(1)} async-done(((bf16[4,128,2048]{2,1,0:T(8,128)(2,1)}), bf16[4,128,2048]{2,1,0:T(8,128)(2,1)S(1)}, u32[]{:S(2)}, u32[]{:S(2)}) %all-to-all-start.1) | async-done | bytes 2097184 | tf_op jit(solution)/shard_map/all_to_all | solution.py:33
  96.3 2.9 %convolution_convert_fusion.1 = bf16[512,512]{1,0:T(8,128)(2,1)S(1)} fusion(bf16[512,2048]{1,0:T(8,128)(2,1)S(1)} %bitcast.31, bf16[1,512,2048]{2,1,0:T(8,128)(2,1)} %param.3), kind=kOutput, calls=%fused_computation.2 | convolution fusion | flops 1074003968 | bytes 4718592 | tf_op jit(solution)/shard_map/dot_general | solution.py:17
  99.2 0.0 collective-permute-done
  99.2 2.9 %broadcast_select_fusion.1 = (bf16[512,512]{1,0:T(8,128)(2,1)S(1)}, bf16[512,512]{1,0:T(8,128)(2,1)S(1)}) fusion(bf16[512,512]{1,0:T(8,128)(2,1)S(1)} %convolution_convert_fusion.1, pred[]{:T(512)S(6)} %eq.3, bf16[512,2048]{1,0:T(8,128)(2,1)S(1)} %bitcast.32, bf16[512,2048]{1,0:T(8,128)(2,1)} %collective-permute-done), kind=kOutput, calls=%fused_computation.7 | convolution fusion | flops 1074528256 | bytes 5767169 | tf_op jit(solution)/shard_map/dot_general | solution.py:17
  102.1 0.1 pad_maximum_fusion
  102.2 35.6 %all_to_all.15 = bf16[32,32,512]{2,1,0:T(8,128)(2,1)S(1)} all-to-all(bf16[32,32,512]{2,1,0:T(8,128)(2,1)S(1)} %bitcast.29), channel_id=1, replica_groups=mesh['zl'=4,'y'=4,'x'=4,'zh'=4,'c'=2] {'zl','y','c'}, dimensions={0} | all-to-all | bytes 2097152 | tf_op jit(solution)/shard_map/all_to_all | solution.py:38
  137.8 0.8 convert_reduce_fusion
Async XLA Ops:
  2.5 12.5 %copy-start = (bf16[1,32,2048]{2,1,0:T(8,128)(2,1)S(1)}, bf16[1,32,2048]{2,1,0:T(8,128)(2,1)}, u32[]{:S(2)}) copy-start(bf16[1,32,2048]{2,1,0:T(8,128)(2,1)} %param.4) | copy-start | bytes 393220
  2.5 39.0 %all-to-all-start = ((bf16[8,64,2048]{2,1,0:T(8,128)(2,1)}), bf16[8,64,2048]{2,1,0:T(8,128)(2,1)S(1)}, u32[]{:S(2)}, u32[]{:S(2)}) async-start(bf16[8,64,2048]{2,1,0:T(8,128)(2,1)} %broadcast_in_dim.15), calls=%async_computation | async-start | bytes 4194304 | tf_op jit(solution)/shard_map/all_to_all | solution.py:25
  13.0 86.2 %collective-permute-start = (bf16[512,2048]{1,0:T(8,128)(2,1)}, bf16[512,2048]{1,0:T(8,128)(2,1)}, u32[]{:S(2)}, u32[]{:S(2)}) collective-permute-start(bf16[512,2048]{1,0:T(8,128)(2,1)} %bitcast.37), channel_id=1, source_target_pairs={{0,1},{1,0},{2,3},{3,2},{4,5},{5,4},{6,7},{7,6},{8,9},{9,8},{10,11... | collective-permute-start | bytes 6291464 | tf_op jit(solution)/shard_map/ppermute | solution.py:27
  70.0 26.3 %all-to-all-start.1 = ((bf16[4,128,2048]{2,1,0:T(8,128)(2,1)}), bf16[4,128,2048]{2,1,0:T(8,128)(2,1)S(1)}, u32[]{:S(2)}, u32[]{:S(2)}) async-start(bf16[4,128,2048]{2,1,0:T(8,128)(2,1)} %broadcast_in_dim.17), calls=%async_computation.1 | async-start | bytes 4194304 | tf_op jit(solution)/shard_map/all_to_all | solution.py:33

commit v3 on v2

v3 whole, which is shorter than its diff:
```python
import jax
import jax.numpy as jnp
from jax import lax
from jax.experimental import pallas as pl
from jax.experimental.pallas import tpu as pltpu
from jax.sharding import Mesh
from jax.sharding import PartitionSpec as P

LAYER = ("zl", "y")
EX = ("x", "zh", "c")
SWAP = [(0, 1), (1, 0)]


def copies(block, n):
    return jnp.broadcast_to(block[None], (n,) + block.shape)


def spread(block_ref, out_ref, sem):
    sent = [pltpu.make_async_copy(block_ref, out_ref.at[n], sem.at[n]) for n in range(8)]
    for copy in sent:
        copy.start()
    for copy in sent:
        copy.wait()


def rows_by_rows(a, b):
    return lax.dot_general(
        a, b, (((1,), (1,)), ((), ())), preferred_element_type=jnp.float32
    )


def condition(query_ref, plane_hbm, out_ref, plane, sems):
    arriving = [
        pltpu.make_async_copy(plane_hbm.at[x], plane.at[x], sems.at[x]) for x in range(4)
    ]
    for copy in arriving:
        copy.start()
    for x in range(4):
        arriving[x].wait()
        out = rows_by_rows(query_ref[...], plane[x])
        out_ref[:, x * 128 : x * 128 + 128] = out.astype(jnp.bfloat16)


def score(conditioned_ref, near_ref, far_hbm, out_ref, far_ref, sem):
    core = lax.axis_index("c")
    rows, k = near_ref.shape
    wide, thin = k // 4, k // 16
    arriving = pltpu.make_async_copy(far_hbm, far_ref, sem)
    arriving.start()
    for side, train_ref in enumerate((near_ref, far_ref)):
        if side == 1:
            arriving.wait()
        owner = core if side == 0 else 1 - core
        for at in range(0, rows, 256):
            train = train_ref[at : at + 256, :]
            total = jnp.zeros((512, 256), jnp.float32)
            for z in range(4):
                columns = [train[:, (x * 4 + z) * thin :][:, :thin] for x in range(4)]
                total += rows_by_rows(
                    conditioned_ref[:, z].reshape(-1, wide), jnp.concatenate(columns, axis=1)
                )
            out_ref[:, owner, :, at : at + 256] = total.astype(jnp.bfloat16).reshape(16, -1, 256)


def on_device(train_grads, query_grads, inverse_fisher):
    train, query, fisher = train_grads[0], query_grads[0], inverse_fisher[0]
    rows, k = train.shape
    mine = query.shape[0]
    eight = pl.pallas_call(
        spread,
        out_shape=jax.ShapeDtypeStruct((8,) + fisher.shape, fisher.dtype),
        in_specs=[pl.BlockSpec(memory_space=pltpu.VMEM)],
        out_specs=pl.BlockSpec(memory_space=pl.ANY),
        scratch_shapes=[pltpu.SemaphoreType.DMA((8,))],
        name="spread",
    )(fisher)
    plane = lax.all_to_all(eight, ("x", "c"), 0, 0)
    plane = plane.reshape(4, -1, k)
    far = lax.ppermute(train, "c", SWAP)
    queries = lax.all_gather(query, "zh", axis=0, tiled=True)
    conditioned = pl.pallas_call(
        condition,
        out_shape=jax.ShapeDtypeStruct((4 * mine, k // 4), jnp.bfloat16),
        in_specs=[pl.BlockSpec(memory_space=pltpu.VMEM), pl.BlockSpec(memory_space=pl.ANY)],
        scratch_shapes=[pltpu.VMEM(plane.shape, jnp.bfloat16), pltpu.SemaphoreType.DMA((4,))],
        compiler_params=pltpu.CompilerParams(vmem_limit_bytes=14 * 2**20),
        cost_estimate=pl.CostEstimate(
            flops=2 * mine * k * k, bytes_accessed=3 * 2**20, transcendentals=0
        ),
        name="condition",
    )(queries, plane)
    conditioned = lax.all_gather(conditioned, "zh", axis=0)
    conditioned, far = lax.optimization_barrier((conditioned, far))
    conditioned = lax.all_to_all(copies(conditioned, 4), "x", 0, 0)
    part = pl.pallas_call(
        score,
        out_shape=jax.ShapeDtypeStruct((16, 2, mine, rows), jnp.bfloat16),
        in_specs=[pl.BlockSpec(memory_space=pltpu.VMEM)] * 2 + [pl.BlockSpec(memory_space=pl.ANY)],
        scratch_shapes=[pltpu.VMEM((rows, k), jnp.bfloat16), pltpu.SemaphoreType.DMA],
        compiler_params=pltpu.CompilerParams(vmem_limit_bytes=14 * 2**20),
        cost_estimate=pl.CostEstimate(
            flops=4 * 16 * mine * rows * k, bytes_accessed=8 * 2**20, transcendentals=0
        ),
        name="score",
    )(conditioned, train, far)
    part = lax.all_to_all(part.reshape(32, mine, rows), LAYER + ("c",), 0, 0)
    total = part.reshape(16, -1, rows).astype(jnp.float32).sum(axis=0)
    return total.T


def solution(mesh):
    split = Mesh(mesh.devices.reshape(4, 4, 4, 4, 2), LAYER + EX)
    spec = P(LAYER, EX, None)
    return jax.shard_map(
        on_device,
        mesh=split,
        in_specs=(spec, spec, spec),
        out_specs=P(EX, LAYER),
        check_vma=False,
    )
```

time: 139 us -> 135 us (0.971)
  blocking collectives: 87.4 us -> 114 us
  waiting for transfers between devices: 22.7 us -> 0.06 us
  Pallas kernels: 0 us -> 7.09 us
  matrix products: 6.58 us -> 0 us
  local copies, waits for them, and re-layouts: 4.82 us -> 0.21 us
  starting transfers between devices: 16.1 us -> 12.5 us
    all_to_all x1 -> x2, blocking collectives: 35.6 us -> 62.1 us  [the longest x1 37.7 us: on_device(): part = lax.all_to_all(part.reshape(32, mine, rows), LAYER + ('c',), 0, 0)]
    all_to_all x2 -> x1, waiting for transfers between devices: 22.7 us -> 0.05 us  [on_device(): plane = lax.all_to_all(eight, ('x', 'c'), 0, 0)]
    all_to_all x2 -> x1, starting transfers between devices: 14.1 us -> 3.7 us  [on_device(): plane = lax.all_to_all(eight, ('x', 'c'), 0, 0)]
    pallas_call x0 -> x3, Pallas kernels: none -> 7.09 us  [the longest x1 2.9 us: on_device(): pl.pallas_call(score, out_shape=jax.ShapeDtypeStruct((16, 2, mine, rows),...]
    ppermute x1, starting transfers between devices: 2.02 us -> 8.78 us  [on_device(): far = lax.ppermute(train, 'c', SWAP)]
    dot_general x3 -> x0, matrix products: 6.58 us -> none  [rows_by_rows(): lax.dot_general(a, b, (((1,), (1,)), ((), ())), preferred_element_type=jn...]
    broadcast_in_dim x3 -> x1, local copies, waits for them, and re-layouts: 4.31 us -> 0.2 us  [copies(): return jnp.broadcast_to(block[None], (n,) + block.shape)]
  transfers between devices with their start and end apart: 3 -> 2, of which waited for: 1 -> 1; matrix products, arithmetic and copies ran while one was open for 4% -> 0% of each run, Pallas kernels for 0% -> 3%
where the time goes in v3:
time: 135 us
  blocking collectives  114 us (84%)
  starting transfers between devices  12.5 us (9%)
  Pallas kernels  7.09 us (5%)
    all_to_all x1, blocking collectives, on_device(): part = lax.all_to_all(part.reshape(32, mine, rows), LAYER + ('c',), 0, 0)  37.7 us
    all_gather x1, blocking collectives, on_device(): queries = lax.all_gather(query, 'zh', axis=0, tiled=True)  26.2 us
    all_gather x1, blocking collectives, on_device(): conditioned = lax.all_gather(conditioned, 'zh', axis=0)  25.7 us
    all_to_all x1, blocking collectives, on_device(): conditioned = lax.all_to_all(copies(conditioned, 4), 'x', 0, 0)  24.5 us
    ppermute x1, starting transfers between devices, on_device(): far = lax.ppermute(train, 'c', SWAP)  8.78 us
    all_to_all x1, starting transfers between devices, on_device(): plane = lax.all_to_all(eight, ('x', 'c'), 0, 0)  3.7 us
    pallas_call x1, Pallas kernels, on_device(): pl.pallas_call(score, out_shape=jax.ShapeDtypeStruct((16, 2, mine, rows),...  2.9 us
  transfers between devices with their start and end apart: 2, of which 1 were waited for; matrix products, arithmetic and copies ran while one was open for 0% of the time, Pallas kernels for 3%

profile of v3, /device:TPU:1, one launch (start us, length us, event | category | flops | bytes accessed | tf_op | source)
XLA Modules:
  0.0 134.8 jit_solution(5507273762410577095)
XLA Ops:
  0.0 8.8 %collective-permute-start = (bf16[512,2048]{1,0:T(8,128)(2,1)}, bf16[512,2048]{1,0:T(8,128)(2,1)}, u32[]{:S(2)}, u32[]{:S(2)}) collective-permute-start(bf16[512,2048]{1,0:T(8,128)(2,1)} %bitcast.14), channel_id=1, source_target_pairs={{0,1},{1,0},{2,3},{3,2},{4,5},{5,4},{6,7},{7,6},{8,9},{9,8},{10,11... | collective-permute-start | bytes 6291464 | tf_op jit(solution)/shard_map/ppermute | solution.py:79
  8.8 2.3 %spread.1 = bf16[8,64,2048]{2,1,0:T(8,128)(2,1)} custom-call(bf16[64,2048]{1,0:T(8,128)(2,1)} %bitcast.18), custom_call_target="tpu_custom_call" | custom-call | tf_op jit(solution)/shard_map/spread/pallas_call | solution.py:69
  11.1 0.0 copy-start.1
  11.1 3.7 %all-to-all-start = ((bf16[8,64,2048]{2,1,0:T(8,128)(2,1)}), bf16[8,64,2048]{2,1,0:T(8,128)(2,1)S(1)}, u32[]{:S(2)}, u32[]{:S(2)}) async-start(bf16[8,64,2048]{2,1,0:T(8,128)(2,1)} %spread.1), calls=%async_computation | async-start | bytes 4194304 | tf_op jit(solution)/shard_map/all_to_all | solution.py:77
  14.8 0.0 copy-done.1
  14.8 26.2 %all-gather = bf16[1,128,2048]{2,1,0:T(8,128)(2,1)S(1)} all-gather(bf16[1,32,2048]{2,1,0:T(8,128)(2,1)S(1)} %copy-done.1), channel_id=2, replica_groups=mesh['zl'=4,'y'=4,'x'=4,'zh'=4,'c'=2] {'zh'}, dimensions={1}, use_global_device_ids=true | all-gather | bytes 655360 | tf_op jit(solution)/shard_map/all_gather | solution.py:80
  41.1 0.1 all-to-all-done
  41.1 1.9 %condition.1 = bf16[128,512]{1,0:T(8,128)(2,1)S(1)} custom-call(bf16[128,2048]{1,0:T(8,128)(2,1)S(1)} %bitcast.12, bf16[4,128,2048]{2,1,0:T(8,128)(2,1)S(1)} %bitcast.11), custom_call_target="tpu_custom_call" | custom-call | flops 268435456 | bytes 3145728 | tf_op jit(solution)/shard_map/condition/pallas_call | solution.py:81
  43.0 25.7 %all-gather.1 = bf16[512,512]{1,0:T(8,128)(2,1)S(1)} all-gather(bf16[128,512]{1,0:T(8,128)(2,1)S(1)} %condition.1), channel_id=3, replica_groups=mesh['zl'=4,'y'=4,'x'=4,'zh'=4,'c'=2] {'zh'}, dimensions={0}, use_global_device_ids=true | all-gather | bytes 655360 | tf_op jit(solution)/shard_map/all_gather | solution.py:92
  68.7 0.0 collective-permute-done.far_hbm
  68.7 0.2 broadcast_in_dim.2
  68.9 0.0 copy-start
  68.9 24.5 %all_to_all.15.conditioned_ref = bf16[4,4,128,512]{3,2,1,0:T(8,128)(2,1)S(1)} all-to-all(bf16[4,4,128,512]{3,2,1,0:T(8,128)(2,1)S(1)} %broadcast_in_dim.2), channel_id=1, replica_groups=mesh['zl'=4,'y'=4,'x'=4,'zh'=4,'c'=2] {'x'}, dimensions={0} | all-to-all | bytes 4194304 | tf_op jit(solution)/shard_map/all_to_all | solution.py:94
  93.4 0.0 copy-done
  93.4 2.9 %score.1 = bf16[16,2,32,512]{3,2,1,0:T(8,128)(2,1)S(1)} custom-call(bf16[4,4,128,512]{3,2,1,0:T(8,128)(2,1)S(1)} %all_to_all.15.conditioned_ref, bf16[512,2048]{1,0:T(8,128)(2,1)S(1)} %bitcast.15, bf16[512,2048]{1,0:T(8,128)(2,1)} %collective-permute-done.far_hbm), custom_call_target="tpu_custom_call" | custom-call | flops 2147483648 | bytes 8388608 | tf_op jit(solution)/shard_map/score/pallas_call | solution.py:95
  96.3 37.7 %all_to_all.16 = bf16[32,32,512]{2,1,0:T(8,128)(2,1)S(1)} all-to-all(bf16[32,32,512]{2,1,0:T(8,128)(2,1)S(1)} %bitcast.13), channel_id=1, replica_groups=mesh['zl'=4,'y'=4,'x'=4,'zh'=4,'c'=2] {'zl','y','c'}, dimensions={0} | all-to-all | bytes 2097152 | tf_op jit(solution)/shard_map/all_to_all | solution.py:106
  134.0 0.8 convert_reduce_fusion
Async XLA Ops:
  0.0 68.7 %collective-permute-start = (bf16[512,2048]{1,0:T(8,128)(2,1)}, bf16[512,2048]{1,0:T(8,128)(2,1)}, u32[]{:S(2)}, u32[]{:S(2)}) collective-permute-start(bf16[512,2048]{1,0:T(8,128)(2,1)} %bitcast.14), channel_id=1, source_target_pairs={{0,1},{1,0},{2,3},{3,2},{4,5},{5,4},{6,7},{7,6},{8,9},{9,8},{10,11... | collective-permute-start | bytes 6291464 | tf_op jit(solution)/shard_map/ppermute | solution.py:79
  11.1 3.7 %copy-start.1 = (bf16[1,32,2048]{2,1,0:T(8,128)(2,1)S(1)}, bf16[1,32,2048]{2,1,0:T(8,128)(2,1)}, u32[]{:S(2)}) copy-start(bf16[1,32,2048]{2,1,0:T(8,128)(2,1)} %param.4) | copy-start | bytes 393220
  11.1 30.0 %all-to-all-start = ((bf16[8,64,2048]{2,1,0:T(8,128)(2,1)}), bf16[8,64,2048]{2,1,0:T(8,128)(2,1)S(1)}, u32[]{:S(2)}, u32[]{:S(2)}) async-start(bf16[8,64,2048]{2,1,0:T(8,128)(2,1)} %spread.1), calls=%async_computation | async-start | bytes 4194304 | tf_op jit(solution)/shard_map/all_to_all | solution.py:77
  68.9 24.5 %copy-start = (bf16[1,512,2048]{2,1,0:T(8,128)(2,1)S(1)}, bf16[1,512,2048]{2,1,0:T(8,128)(2,1)}, u32[]{:S(2)}) copy-start(bf16[1,512,2048]{2,1,0:T(8,128)(2,1)} %param.3) | copy-start | bytes 6291460

commit v4 on v3

--- a/solution.py
+++ b/solution.py
@@ -6,7 +6,7 @@
 from jax.sharding import Mesh
 from jax.sharding import PartitionSpec as P
 
-LAYER = ("zl", "y")
+LAYER = ("z1", "z0", "y")
 EX = ("x", "zh", "c")
 SWAP = [(0, 1), (1, 0)]
 
@@ -59,7 +59,19 @@
                 total += rows_by_rows(
                     conditioned_ref[:, z].reshape(-1, wide), jnp.concatenate(columns, axis=1)
                 )
-            out_ref[:, owner, :, at : at + 256] = total.astype(jnp.bfloat16).reshape(16, -1, 256)
+            total = total.astype(jnp.bfloat16).reshape(2, 2, 4, -1, 256)
+            for z1 in range(2):
+                out_ref[:, :, owner, z1, :, at : at + 256] = total[z1]
+
+
+def sum_layers(part_ref, keep_ref, send_ref):
+    mine = lax.axis_index("z1")
+    for side in range(2):
+        for out_ref, z1 in ((keep_ref, mine), (send_ref, 1 - mine)):
+            total = part_ref[0, side, z1].astype(jnp.float32)
+            for n in range(1, 8):
+                total += part_ref[n, side, z1].astype(jnp.float32)
+            out_ref[side] = total.astype(out_ref.dtype)
 
 
 def on_device(train_grads, query_grads, inverse_fisher):
@@ -94,7 +106,7 @@
     conditioned = lax.all_to_all(copies(conditioned, 4), "x", 0, 0)
     part = pl.pallas_call(
         score,
-        out_shape=jax.ShapeDtypeStruct((16, 2, mine, rows), jnp.bfloat16),
+        out_shape=jax.ShapeDtypeStruct((2, 4, 2, 2, mine, rows), jnp.bfloat16),
         in_specs=[pl.BlockSpec(memory_space=pltpu.VMEM)] * 2 + [pl.BlockSpec(memory_space=pl.ANY)],
         scratch_shapes=[pltpu.VMEM((rows, k), jnp.bfloat16), pltpu.SemaphoreType.DMA],
         compiler_params=pltpu.CompilerParams(vmem_limit_bytes=14 * 2**20),
@@ -103,13 +115,22 @@
         ),
         name="score",
     )(conditioned, train, far)
-    part = lax.all_to_all(part.reshape(32, mine, rows), LAYER + ("c",), 0, 0)
-    total = part.reshape(16, -1, rows).astype(jnp.float32).sum(axis=0)
-    return total.T
+    part = lax.all_to_all(part.reshape(16, 2, mine, rows), ("z0", "y", "c"), 0, 0)
+    keep, send = pl.pallas_call(
+        sum_layers,
+        out_shape=(
+            jax.ShapeDtypeStruct((2, mine, rows), jnp.float32),
+            jax.ShapeDtypeStruct((2, mine, rows), jnp.bfloat16),
+        ),
+        compiler_params=pltpu.CompilerParams(vmem_limit_bytes=14 * 2**20),
+        name="sum_layers",
+    )(part.reshape(8, 2, 2, mine, rows))
+    total = keep + lax.ppermute(send, "z1", SWAP).astype(jnp.float32)
+    return total.reshape(2 * mine, rows).T
 
 
 def solution(mesh):
-    split = Mesh(mesh.devices.reshape(4, 4, 4, 4, 2), LAYER + EX)
+    split = Mesh(mesh.devices.reshape(2, 2, 4, 4, 4, 2), LAYER + EX)
     spec = P(LAYER, EX, None)
     return jax.shard_map(
         on_device,

time: 135 us -> 130 us (0.963)
  blocking collectives: 114 us -> 102 us
  starting transfers between devices: 12.5 us -> 15.8 us
  waiting for transfers between devices: 0.06 us -> 3.33 us
    all_to_all x1, blocking collectives: 37.7 us -> 24.5 us  [on_device(): lax.all_to_all(part.reshape(16, 2, mine, rows), ('z0', 'y', 'c'), 0, 0)]
    ppermute x0 -> x1, starting transfers between devices: none -> 3.33 us  [on_device(): total = keep + lax.ppermute(send, 'z1', SWAP).astype(jnp.float32)]
    ppermute x0 -> x1, waiting for transfers between devices: none -> 3.27 us  [on_device(): total = keep + lax.ppermute(send, 'z1', SWAP).astype(jnp.float32)]
    pallas_call x1 -> x2, Pallas kernels: 2.9 us -> 3.03 us  [the longest x1 2.9 us: on_device(): pl.pallas_call(score, out_shape=jax.ShapeDtypeStruct((2, 4, 2, 2, mine, r...]
  transfers between devices with their start and end apart: 2 -> 3, of which waited for: 1 -> 2; matrix products, arithmetic and copies ran while one was open for 0% -> 0% of each run, Pallas kernels for 3% -> 3%
where the time goes in v4:
time: 130 us; the launch traced here: 129 us
  blocking collectives  102 us (78%)
  starting transfers between devices  15.8 us (12%)
  Pallas kernels  7.23 us (6%)
  waiting for transfers between devices  3.33 us (3%)
    all_gather x1, blocking collectives, on_device(): queries = lax.all_gather(query, 'zh', axis=0, tiled=True)  26.2 us
    all_gather x1, blocking collectives, on_device(): conditioned = lax.all_gather(conditioned, 'zh', axis=0)  25.8 us
    all_to_all x1, blocking collectives, on_device(): conditioned = lax.all_to_all(copies(conditioned, 4), 'x', 0, 0)  25.3 us
    all_to_all x1, blocking collectives, on_device(): lax.all_to_all(part.reshape(16, 2, mine, rows), ('z0', 'y', 'c'), 0, 0)  24.5 us
    ppermute x1, starting transfers between devices, on_device(): far = lax.ppermute(train, 'c', SWAP)  8.78 us
    all_to_all x1, starting transfers between devices, on_device(): plane = lax.all_to_all(eight, ('x', 'c'), 0, 0)  3.7 us
    ppermute x1, starting transfers between devices, on_device(): total = keep + lax.ppermute(send, 'z1', SWAP).astype(jnp.float32)  3.33 us
    ppermute x1, waiting for transfers between devices, on_device(): total = keep + lax.ppermute(send, 'z1', SWAP).astype(jnp.float32)  3.27 us
  transfers between devices with their start and end apart: 3, of which 2 were waited for; matrix products, arithmetic and copies ran while one was open for 0% of the time, Pallas kernels for 3%

profile of v4, /device:TPU:1, one launch (start us, length us, event | category | flops | bytes accessed | tf_op | source)
XLA Modules:
  0.0 129.1 jit_solution(9579925092433397742)
XLA Ops:
  0.0 8.8 %collective-permute-start = (bf16[512,2048]{1,0:T(8,128)(2,1)}, bf16[512,2048]{1,0:T(8,128)(2,1)}, u32[]{:S(2)}, u32[]{:S(2)}) collective-permute-start(bf16[512,2048]{1,0:T(8,128)(2,1)} %bitcast.14), channel_id=1, source_target_pairs={{0,1},{1,0},{2,3},{3,2},{4,5},{5,4},{6,7},{7,6},{8,9},{9,8},{10,11... | collective-permute-start | bytes 6291464 | tf_op jit(solution)/shard_map/ppermute | solution.py:91
  8.8 2.3 %spread.1 = bf16[8,64,2048]{2,1,0:T(8,128)(2,1)} custom-call(bf16[64,2048]{1,0:T(8,128)(2,1)} %bitcast.17), custom_call_target="tpu_custom_call" | custom-call | tf_op jit(solution)/shard_map/spread/pallas_call | solution.py:81
  11.1 0.0 copy-start.1
  11.1 3.7 %all-to-all-start = ((bf16[8,64,2048]{2,1,0:T(8,128)(2,1)}), bf16[8,64,2048]{2,1,0:T(8,128)(2,1)S(1)}, u32[]{:S(2)}, u32[]{:S(2)}) async-start(bf16[8,64,2048]{2,1,0:T(8,128)(2,1)} %spread.1), calls=%async_computation | async-start | bytes 4194304 | tf_op jit(solution)/shard_map/all_to_all | solution.py:89
  14.8 0.0 copy-done.1
  14.9 26.2 %all-gather = bf16[1,128,2048]{2,1,0:T(8,128)(2,1)S(1)} all-gather(bf16[1,32,2048]{2,1,0:T(8,128)(2,1)S(1)} %copy-done.1), channel_id=2, replica_groups=mesh['z1'=2,'z0'=2,'y'=4,'x'=4,'zh'=4,'c'=2] {'zh'}, dimensions={1}, use_global_device_ids=true | all-gather | bytes 655360 | tf_op jit(solution)/shard_map/all_gather | solution.py:92
  41.1 0.1 all-to-all-done
  41.2 1.9 %condition.1 = bf16[128,512]{1,0:T(8,128)(2,1)S(1)} custom-call(bf16[128,2048]{1,0:T(8,128)(2,1)S(1)} %bitcast.12, bf16[4,128,2048]{2,1,0:T(8,128)(2,1)S(1)} %bitcast.10), custom_call_target="tpu_custom_call" | custom-call | flops 268435456 | bytes 3145728 | tf_op jit(solution)/shard_map/condition/pallas_call | solution.py:93
  43.0 25.8 %all-gather.1 = bf16[512,512]{1,0:T(8,128)(2,1)S(1)} all-gather(bf16[128,512]{1,0:T(8,128)(2,1)S(1)} %condition.1), channel_id=3, replica_groups=mesh['z1'=2,'z0'=2,'y'=4,'x'=4,'zh'=4,'c'=2] {'zh'}, dimensions={0}, use_global_device_ids=true | all-gather | bytes 655360 | tf_op jit(solution)/shard_map/all_gather | solution.py:104
  68.8 0.0 collective-permute-done.far_hbm
  68.8 0.2 broadcast_in_dim.2
  69.0 0.0 copy-start
  69.0 25.3 %all_to_all.15.conditioned_ref = bf16[4,4,128,512]{3,2,1,0:T(8,128)(2,1)S(1)} all-to-all(bf16[4,4,128,512]{3,2,1,0:T(8,128)(2,1)S(1)} %broadcast_in_dim.2), channel_id=1, replica_groups=mesh['z1'=2,'z0'=2,'y'=4,'x'=4,'zh'=4,'c'=2] {'x'}, dimensions={0} | all-to-all | bytes 4194304 | tf_op jit(solution)/shard_map/all_to_all | solution.py:106
  94.3 0.0 copy-done
  94.3 2.9 %score.1 = bf16[2,4,2,2,32,512]{5,4,3,2,1,0:T(8,128)(2,1)S(1)} custom-call(bf16[4,4,128,512]{3,2,1,0:T(8,128)(2,1)S(1)} %all_to_all.15.conditioned_ref, bf16[512,2048]{1,0:T(8,128)(2,1)S(1)} %bitcast.15, bf16[512,2048]{1,0:T(8,128)(2,1)} %collective-permute-done.far_hbm), custom_call_target="tpu_custom_call" | custom-call | flops 2147483648 | bytes 8388608 | tf_op jit(solution)/shard_map/score/pallas_call | solution.py:107
  97.2 24.5 %all_to_all.16 = bf16[16,2,32,512]{3,2,1,0:T(8,128)(2,1)S(1)} all-to-all(bf16[16,2,32,512]{3,2,1,0:T(8,128)(2,1)S(1)} %bitcast.13), channel_id=1, replica_groups=mesh['z1'=2,'z0'=2,'y'=4,'x'=4,'zh'=4,'c'=2] {'z0','y','c'}, dimensions={0} | all-to-all | bytes 2097152 | tf_op jit(solution)/shard_map/all_to_all | solution.py:118
  121.7 0.1 sum_layers.1
  121.8 3.3 %collective-permute-start.1 = (bf16[2,32,512]{2,1,0:T(8,128)(2,1)S(1)}, bf16[2,32,512]{2,1,0:T(8,128)(2,1)S(1)}, u32[]{:S(2)}, u32[]{:S(2)}) collective-permute-start(bf16[2,32,512]{2,1,0:T(8,128)(2,1)S(1)} %get-tuple-element.12), channel_id=1, source_target_pairs={{0,256},{256,0},{1,257},{257,1},{2,258},{258,2},{3,259},{259,3},{4... | collective-permute-start | bytes 196616 | tf_op jit(solution)/shard_map/ppermute | solution.py:128
  125.2 3.3 %collective-permute-done.1 = bf16[2,32,512]{2,1,0:T(8,128)(2,1)S(1)} collective-permute-done((bf16[2,32,512]{2,1,0:T(8,128)(2,1)S(1)}, bf16[2,32,512]{2,1,0:T(8,128)(2,1)S(1)}, u32[]{:S(2)}, u32[]{:S(2)}) %collective-permute-start.1) | collective-permute-done | bytes 65568 | tf_op jit(solution)/shard_map/ppermute | solution.py:128
  128.5 0.7 convert_add_fusion
Async XLA Ops:
  0.0 68.8 %collective-permute-start = (bf16[512,2048]{1,0:T(8,128)(2,1)}, bf16[512,2048]{1,0:T(8,128)(2,1)}, u32[]{:S(2)}, u32[]{:S(2)}) collective-permute-start(bf16[512,2048]{1,0:T(8,128)(2,1)} %bitcast.14), channel_id=1, source_target_pairs={{0,1},{1,0},{2,3},{3,2},{4,5},{5,4},{6,7},{7,6},{8,9},{9,8},{10,11... | collective-permute-start | bytes 6291464 | tf_op jit(solution)/shard_map/ppermute | solution.py:91
  11.1 3.7 %copy-start.1 = (bf16[1,32,2048]{2,1,0:T(8,128)(2,1)S(1)}, bf16[1,32,2048]{2,1,0:T(8,128)(2,1)}, u32[]{:S(2)}) copy-start(bf16[1,32,2048]{2,1,0:T(8,128)(2,1)} %param.4) | copy-start | bytes 393220
  11.1 30.0 %all-to-all-start = ((bf16[8,64,2048]{2,1,0:T(8,128)(2,1)}), bf16[8,64,2048]{2,1,0:T(8,128)(2,1)S(1)}, u32[]{:S(2)}, u32[]{:S(2)}) async-start(bf16[8,64,2048]{2,1,0:T(8,128)(2,1)} %spread.1), calls=%async_computation | async-start | bytes 4194304 | tf_op jit(solution)/shard_map/all_to_all | solution.py:89
  69.0 25.3 %copy-start = (bf16[1,512,2048]{2,1,0:T(8,128)(2,1)S(1)}, bf16[1,512,2048]{2,1,0:T(8,128)(2,1)}, u32[]{:S(2)}) copy-start(bf16[1,512,2048]{2,1,0:T(8,128)(2,1)} %param.3) | copy-start | bytes 6291460
  121.8 6.6 %collective-permute-start.1 = (bf16[2,32,512]{2,1,0:T(8,128)(2,1)S(1)}, bf16[2,32,512]{2,1,0:T(8,128)(2,1)S(1)}, u32[]{:S(2)}, u32[]{:S(2)}) collective-permute-start(bf16[2,32,512]{2,1,0:T(8,128)(2,1)S(1)} %get-tuple-element.12), channel_id=1, source_target_pairs={{0,256},{256,0},{1,257},{257,1},{2,258},{258,2},{3,259},{259,3},{4... | collective-permute-start | bytes 196616 | tf_op jit(solution)/shard_map/ppermute | solution.py:128

commit v5 on v4

--- a/solution.py
+++ b/solution.py
@@ -29,15 +29,9 @@
     )
 
 
-def condition(query_ref, plane_hbm, out_ref, plane, sems):
-    arriving = [
-        pltpu.make_async_copy(plane_hbm.at[x], plane.at[x], sems.at[x]) for x in range(4)
-    ]
-    for copy in arriving:
-        copy.start()
+def condition(query_ref, plane_ref, out_ref):
     for x in range(4):
-        arriving[x].wait()
-        out = rows_by_rows(query_ref[...], plane[x])
+        out = rows_by_rows(query_ref[...], plane_ref[x])
         out_ref[:, x * 128 : x * 128 + 128] = out.astype(jnp.bfloat16)
 
 
@@ -93,9 +87,7 @@
     conditioned = pl.pallas_call(
         condition,
         out_shape=jax.ShapeDtypeStruct((4 * mine, k // 4), jnp.bfloat16),
-        in_specs=[pl.BlockSpec(memory_space=pltpu.VMEM), pl.BlockSpec(memory_space=pl.ANY)],
-        scratch_shapes=[pltpu.VMEM(plane.shape, jnp.bfloat16), pltpu.SemaphoreType.DMA((4,))],
-        compiler_params=pltpu.CompilerParams(vmem_limit_bytes=14 * 2**20),
+                compiler_params=pltpu.CompilerParams(vmem_limit_bytes=14 * 2**20),
         cost_estimate=pl.CostEstimate(
             flops=2 * mine * k * k, bytes_accessed=3 * 2**20, transcendentals=0
         ),

time: 130 us -> 128 us (0.985)
  transfers between devices with their start and end apart: 3 -> 3, of which waited for: 2 -> 2; matrix products, arithmetic and copies ran while one was open for 0% -> 0% of each run, Pallas kernels for 3% -> 2%
where the time goes in v5:
time: 128 us
  blocking collectives  102 us (80%)
  starting transfers between devices  15.9 us (12%)
  Pallas kernels  6.07 us (5%)
  waiting for transfers between devices  3.24 us (3%)
    all_gather x1, blocking collectives, on_device(): queries = lax.all_gather(query, 'zh', axis=0, tiled=True)  26.2 us
    all_gather x1, blocking collectives, on_device(): conditioned = lax.all_gather(conditioned, 'zh', axis=0)  25.8 us
    all_to_all x1, blocking collectives, on_device(): conditioned = lax.all_to_all(copies(conditioned, 4), 'x', 0, 0)  25.1 us
    all_to_all x1, blocking collectives, on_device(): lax.all_to_all(part.reshape(16, 2, mine, rows), ('z0', 'y', 'c'), 0, 0)  24.7 us
    ppermute x1, starting transfers between devices, on_device(): far = lax.ppermute(train, 'c', SWAP)  8.78 us
    all_to_all x1, starting transfers between devices, on_device(): plane = lax.all_to_all(eight, ('x', 'c'), 0, 0)  3.7 us
    ppermute x1, starting transfers between devices, on_device(): total = keep + lax.ppermute(send, 'z1', SWAP).astype(jnp.float32)  3.42 us
    ppermute x1, waiting for transfers between devices, on_device(): total = keep + lax.ppermute(send, 'z1', SWAP).astype(jnp.float32)  3.18 us
  transfers between devices with their start and end apart: 3, of which 2 were waited for; matrix products, arithmetic and copies ran while one was open for 0% of the time, Pallas kernels for 2%

profile of v5, /device:TPU:1, one launch (start us, length us, event | category | flops | bytes accessed | tf_op | source)
XLA Modules:
  0.0 127.9 jit_solution(15407382875536953887)
XLA Ops:
  0.0 8.8 %collective-permute-start = (bf16[512,2048]{1,0:T(8,128)(2,1)}, bf16[512,2048]{1,0:T(8,128)(2,1)}, u32[]{:S(2)}, u32[]{:S(2)}) collective-permute-start(bf16[512,2048]{1,0:T(8,128)(2,1)} %bitcast.14), channel_id=1, source_target_pairs={{0,1},{1,0},{2,3},{3,2},{4,5},{5,4},{6,7},{7,6},{8,9},{9,8},{10,11... | collective-permute-start | bytes 6291464 | tf_op jit(solution)/shard_map/ppermute | solution.py:85
  8.8 2.3 %spread.1 = bf16[8,64,2048]{2,1,0:T(8,128)(2,1)} custom-call(bf16[64,2048]{1,0:T(8,128)(2,1)} %bitcast.17), custom_call_target="tpu_custom_call" | custom-call | tf_op jit(solution)/shard_map/spread/pallas_call | solution.py:75
  11.1 0.0 copy-start.1
  11.1 3.7 %all-to-all-start = ((bf16[8,64,2048]{2,1,0:T(8,128)(2,1)}), bf16[8,64,2048]{2,1,0:T(8,128)(2,1)S(1)}, u32[]{:S(2)}, u32[]{:S(2)}) async-start(bf16[8,64,2048]{2,1,0:T(8,128)(2,1)} %spread.1), calls=%async_computation | async-start | bytes 4194304 | tf_op jit(solution)/shard_map/all_to_all | solution.py:83
  14.8 0.0 copy-done.1
  14.9 26.2 %all-gather = bf16[1,128,2048]{2,1,0:T(8,128)(2,1)S(1)} all-gather(bf16[1,32,2048]{2,1,0:T(8,128)(2,1)S(1)} %copy-done.1), channel_id=2, replica_groups=mesh['z1'=2,'z0'=2,'y'=4,'x'=4,'zh'=4,'c'=2] {'zh'}, dimensions={1}, use_global_device_ids=true | all-gather | bytes 655360 | tf_op jit(solution)/shard_map/all_gather | solution.py:86
  41.1 0.1 all-to-all-done
  41.2 0.7 condition.1
  41.9 25.8 %all-gather.1 = bf16[512,512]{1,0:T(8,128)(2,1)S(1)} all-gather(bf16[128,512]{1,0:T(8,128)(2,1)S(1)} %condition.1), channel_id=3, replica_groups=mesh['z1'=2,'z0'=2,'y'=4,'x'=4,'zh'=4,'c'=2] {'zh'}, dimensions={0}, use_global_device_ids=true | all-gather | bytes 655360 | tf_op jit(solution)/shard_map/all_gather | solution.py:96
  67.6 0.0 collective-permute-done.far_hbm
  67.7 0.2 broadcast_in_dim.2
  67.9 0.0 copy-start
  67.9 25.1 %all_to_all.15.conditioned_ref = bf16[4,4,128,512]{3,2,1,0:T(8,128)(2,1)S(1)} all-to-all(bf16[4,4,128,512]{3,2,1,0:T(8,128)(2,1)S(1)} %broadcast_in_dim.2), channel_id=1, replica_groups=mesh['z1'=2,'z0'=2,'y'=4,'x'=4,'zh'=4,'c'=2] {'x'}, dimensions={0} | all-to-all | bytes 4194304 | tf_op jit(solution)/shard_map/all_to_all | solution.py:98
  92.9 0.0 copy-done
  92.9 2.9 %score.1 = bf16[2,4,2,2,32,512]{5,4,3,2,1,0:T(8,128)(2,1)S(1)} custom-call(bf16[4,4,128,512]{3,2,1,0:T(8,128)(2,1)S(1)} %all_to_all.15.conditioned_ref, bf16[512,2048]{1,0:T(8,128)(2,1)S(1)} %bitcast.15, bf16[512,2048]{1,0:T(8,128)(2,1)} %collective-permute-done.far_hbm), custom_call_target="tpu_custom_call" | custom-call | flops 2147483648 | bytes 8388608 | tf_op jit(solution)/shard_map/score/pallas_call | solution.py:99
  95.8 24.7 %all_to_all.16 = bf16[16,2,32,512]{3,2,1,0:T(8,128)(2,1)S(1)} all-to-all(bf16[16,2,32,512]{3,2,1,0:T(8,128)(2,1)S(1)} %bitcast.13), channel_id=1, replica_groups=mesh['z1'=2,'z0'=2,'y'=4,'x'=4,'zh'=4,'c'=2] {'z0','y','c'}, dimensions={0} | all-to-all | bytes 2097152 | tf_op jit(solution)/shard_map/all_to_all | solution.py:110
  120.5 0.1 sum_layers.1
  120.6 3.4 %collective-permute-start.1 = (bf16[2,32,512]{2,1,0:T(8,128)(2,1)S(1)}, bf16[2,32,512]{2,1,0:T(8,128)(2,1)S(1)}, u32[]{:S(2)}, u32[]{:S(2)}) collective-permute-start(bf16[2,32,512]{2,1,0:T(8,128)(2,1)S(1)} %get-tuple-element.12), channel_id=1, source_target_pairs={{0,256},{256,0},{1,257},{257,1},{2,258},{258,2},{3,259},{259,3},{4... | collective-permute-start | bytes 196616 | tf_op jit(solution)/shard_map/ppermute | solution.py:120
  124.1 3.2 %collective-permute-done.1 = bf16[2,32,512]{2,1,0:T(8,128)(2,1)S(1)} collective-permute-done((bf16[2,32,512]{2,1,0:T(8,128)(2,1)S(1)}, bf16[2,32,512]{2,1,0:T(8,128)(2,1)S(1)}, u32[]{:S(2)}, u32[]{:S(2)}) %collective-permute-start.1) | collective-permute-done | bytes 65568 | tf_op jit(solution)/shard_map/ppermute | solution.py:120
  127.2 0.7 convert_add_fusion
Async XLA Ops:
  0.0 67.7 %collective-permute-start = (bf16[512,2048]{1,0:T(8,128)(2,1)}, bf16[512,2048]{1,0:T(8,128)(2,1)}, u32[]{:S(2)}, u32[]{:S(2)}) collective-permute-start(bf16[512,2048]{1,0:T(8,128)(2,1)} %bitcast.14), channel_id=1, source_target_pairs={{0,1},{1,0},{2,3},{3,2},{4,5},{5,4},{6,7},{7,6},{8,9},{9,8},{10,11... | collective-permute-start | bytes 6291464 | tf_op jit(solution)/shard_map/ppermute | solution.py:85
  11.1 3.7 %copy-start.1 = (bf16[1,32,2048]{2,1,0:T(8,128)(2,1)S(1)}, bf16[1,32,2048]{2,1,0:T(8,128)(2,1)}, u32[]{:S(2)}) copy-start(bf16[1,32,2048]{2,1,0:T(8,128)(2,1)} %param.4) | copy-start | bytes 393220
  11.1 30.0 %all-to-all-start = ((bf16[8,64,2048]{2,1,0:T(8,128)(2,1)}), bf16[8,64,2048]{2,1,0:T(8,128)(2,1)S(1)}, u32[]{:S(2)}, u32[]{:S(2)}) async-start(bf16[8,64,2048]{2,1,0:T(8,128)(2,1)} %spread.1), calls=%async_computation | async-start | bytes 4194304 | tf_op jit(solution)/shard_map/all_to_all | solution.py:83
  67.9 25.1 %copy-start = (bf16[1,512,2048]{2,1,0:T(8,128)(2,1)S(1)}, bf16[1,512,2048]{2,1,0:T(8,128)(2,1)}, u32[]{:S(2)}) copy-start(bf16[1,512,2048]{2,1,0:T(8,128)(2,1)} %param.3) | copy-start | bytes 6291460
  120.6 6.6 %collective-permute-start.1 = (bf16[2,32,512]{2,1,0:T(8,128)(2,1)S(1)}, bf16[2,32,512]{2,1,0:T(8,128)(2,1)S(1)}, u32[]{:S(2)}, u32[]{:S(2)}) collective-permute-start(bf16[2,32,512]{2,1,0:T(8,128)(2,1)S(1)} %get-tuple-element.12), channel_id=1, source_target_pairs={{0,256},{256,0},{1,257},{257,1},{2,258},{258,2},{3,259},{259,3},{4... | collective-permute-start | bytes 196616 | tf_op jit(solution)/shard_map/ppermute | solution.py:120

commit v6 on v5

--- a/solution.py
+++ b/solution.py
@@ -35,27 +35,68 @@
         out_ref[:, x * 128 : x * 128 + 128] = out.astype(jnp.bfloat16)
 
 
-def score(conditioned_ref, near_ref, far_hbm, out_ref, far_ref, sem):
+OWN = ((0, 0), (0, 1))
+SIDES = ((3, 0), (1, 1), (3, 1), (1, 0))
+OPPOSITE = ((2, 0), (2, 1))
+
+
+def shift_x(block, by):
+    return lax.ppermute(block, "x", [(i, (i + by) % 4) for i in range(4)])
+
+
+def score(halves, trains, put, arrived=None):
     core = lax.axis_index("c")
-    rows, k = near_ref.shape
-    wide, thin = k // 4, k // 16
-    arriving = pltpu.make_async_copy(far_hbm, far_ref, sem)
-    arriving.start()
-    for side, train_ref in enumerate((near_ref, far_ref)):
-        if side == 1:
-            arriving.wait()
+    rows, k = trains[0].shape
+    thin = k // 16
+    for side, train_ref in enumerate(trains):
+        if side == 1 and arrived is not None:
+            arrived.wait()
         owner = core if side == 0 else 1 - core
         for at in range(0, rows, 256):
             train = train_ref[at : at + 256, :]
-            total = jnp.zeros((512, 256), jnp.float32)
+            total = None
             for z in range(4):
                 columns = [train[:, (x * 4 + z) * thin :][:, :thin] for x in range(4)]
-                total += rows_by_rows(
-                    conditioned_ref[:, z].reshape(-1, wide), jnp.concatenate(columns, axis=1)
+                part = rows_by_rows(
+                    jnp.concatenate([half[z] for half in halves], axis=0),
+                    jnp.concatenate(columns, axis=1),
                 )
-            total = total.astype(jnp.bfloat16).reshape(2, 2, 4, -1, 256)
-            for z1 in range(2):
-                out_ref[:, :, owner, z1, :, at : at + 256] = total[z1]
+                total = part if total is None else total + part
+            put(owner, at, total.astype(jnp.bfloat16).reshape(len(halves), 2, -1, 256))
+
+
+def score_own(first_ref, second_ref, near_ref, far_hbm, out_ref, far_ref, sem):
+    arriving = pltpu.make_async_copy(far_hbm, far_ref, sem)
+    arriving.start()
+
+    def put(owner, at, block):
+        out_ref[:, :, owner, :, at : at + 256] = block
+
+    score((first_ref, second_ref), (near_ref, far_ref), put, arriving)
+
+
+def score_sides(*refs):
+    out_ref = refs[-1]
+
+    def put(owner, at, block):
+        out_ref[:, :, owner, :, at : at + 256] = block
+
+    score(refs[:4], refs[4:6], put)
+
+
+def score_last(first_ref, second_ref, near_ref, far_ref, own_ref, sides_ref, out_ref):
+    x = lax.axis_index("x")
+    for order, scored in ((OWN, own_ref), (SIDES, sides_ref)):
+        for n, (step, half) in enumerate(order):
+            at = lax.rem(x + step, 4)
+            out_ref[lax.rem(at, 2), 2 * half : 2 * half + 2, :, at // 2] = scored[n]
+
+    def put(owner, at, block):
+        to = lax.rem(x + 2, 4)
+        for n, (_, half) in enumerate(OPPOSITE):
+            out_ref[lax.rem(to, 2), 2 * half : 2 * half + 2, owner, to // 2, :, at : at + 256] = block[n]
+
+    score((first_ref, second_ref), (near_ref, far_ref), put)
 
 
 def sum_layers(part_ref, keep_ref, send_ref):
@@ -93,20 +134,44 @@
         ),
         name="condition",
     )(queries, plane)
-    conditioned = lax.all_gather(conditioned, "zh", axis=0)
+    conditioned = lax.all_gather(conditioned.reshape(2, 2 * mine, -1), "zh", axis=1)
     conditioned, far = lax.optimization_barrier((conditioned, far))
-    conditioned = lax.all_to_all(copies(conditioned, 4), "x", 0, 0)
+    first, second = conditioned[0], conditioned[1]
+    behind_first, ahead_second = shift_x(first, 1), shift_x(second, -1)
+    behind_second, ahead_first = shift_x(second, 1), shift_x(first, -1)
+    opposite_first, opposite_second = shift_x(behind_first, 1), shift_x(ahead_second, -1)
+
+    def options(n):
+        return dict(
+            compiler_params=pltpu.CompilerParams(vmem_limit_bytes=14 * 2**20),
+            cost_estimate=pl.CostEstimate(
+                flops=8 * n * mine * rows * k, bytes_accessed=6 * 2**20, transcendentals=0
+            ),
+        )
+
+    own, far = pl.pallas_call(
+        score_own,
+        out_shape=(
+            jax.ShapeDtypeStruct((2, 2, 2, mine, rows), jnp.bfloat16),
+            jax.ShapeDtypeStruct((rows, k), jnp.bfloat16),
+        ),
+        in_specs=[pl.BlockSpec(memory_space=pltpu.VMEM)] * 3 + [pl.BlockSpec(memory_space=pl.ANY)],
+        scratch_shapes=[pltpu.SemaphoreType.DMA],
+        name="score_own",
+        **options(2),
+    )(first, second, train, far)
+    sides = pl.pallas_call(
+        score_sides,
+        out_shape=jax.ShapeDtypeStruct((4, 2, 2, mine, rows), jnp.bfloat16),
+        name="score_sides",
+        **options(4),
+    )(behind_first, ahead_second, behind_second, ahead_first, train, far)
     part = pl.pallas_call(
-        score,
+        score_last,
         out_shape=jax.ShapeDtypeStruct((2, 4, 2, 2, mine, rows), jnp.bfloat16),
-        in_specs=[pl.BlockSpec(memory_space=pltpu.VMEM)] * 2 + [pl.BlockSpec(memory_space=pl.ANY)],
-        scratch_shapes=[pltpu.VMEM((rows, k), jnp.bfloat16), pltpu.SemaphoreType.DMA],
-        compiler_params=pltpu.CompilerParams(vmem_limit_bytes=14 * 2**20),
-        cost_estimate=pl.CostEstimate(
-            flops=4 * 16 * mine * rows * k, bytes_accessed=8 * 2**20, transcendentals=0
-        ),
-        name="score",
-    )(conditioned, train, far)
+        name="score_last",
+        **options(2),
+    )(opposite_first, opposite_second, train, far, own, sides)
     part = lax.all_to_all(part.reshape(16, 2, mine, rows), ("z0", "y", "c"), 0, 0)
     keep, send = pl.pallas_call(
         sum_layers,

time: 128 us -> 128 us (level)
  blocking collectives: 102 us -> 78.7 us
  starting transfers between devices: 15.9 us -> 34.1 us
  Pallas kernels: 6.07 us -> 8.41 us
  waiting for transfers between devices: 3.24 us -> 5.24 us
    all_to_all x1 -> x0, blocking collectives: 25.1 us -> none  [on_device(): conditioned = lax.all_to_all(copies(conditioned, 4), 'x', 0, 0)]
    ppermute x0 -> x6, starting transfers between devices: none -> 17.1 us  [shift_x(): return lax.ppermute(block, 'x', [(i, (i + by) % 4) for i in range(4)])]
    pallas_call x1 -> x3, Pallas kernels: 2.9 us -> 5.23 us  [the longest x1 2.43 us: on_device(): pl.pallas_call(score_own, out_shape=(jax.ShapeDtypeStruct((2, 2, 2, mine,...]
    all_to_all x1, blocking collectives: 24.7 us -> 26.6 us  [on_device(): lax.all_to_all(part.reshape(16, 2, mine, rows), ('z0', 'y', 'c'), 0, 0)]
    ppermute x0 -> x6, waiting for transfers between devices: none -> 1.83 us  [shift_x(): return lax.ppermute(block, 'x', [(i, (i + by) % 4) for i in range(4)])]
  transfers between devices with their start and end apart: 3 -> 9, of which waited for: 2 -> 4; matrix products, arithmetic and copies ran while one was open for 0% -> 0% of each run, Pallas kernels for 2% -> 5%
where the time goes in v6:
time: 128 us; the launch traced here: 127 us
  blocking collectives  78.7 us (61%)
  starting transfers between devices  34.1 us (27%)
  Pallas kernels  8.41 us (7%)
  waiting for transfers between devices  5.24 us (4%)
    all_to_all x1, blocking collectives, on_device(): lax.all_to_all(part.reshape(16, 2, mine, rows), ('z0', 'y', 'c'), 0, 0)  26.6 us
    all_gather x1, blocking collectives, on_device(): queries = lax.all_gather(query, 'zh', axis=0, tiled=True)  26.2 us
    all_gather x1, blocking collectives, on_device(): lax.all_gather(conditioned.reshape(2, 2 * mine, -1), 'zh', axis=1)  25.8 us
    ppermute x6, starting transfers between devices, shift_x(): return lax.ppermute(block, 'x', [(i, (i + by) % 4) for i in range(4)])  17.1 us
    ppermute x1, starting transfers between devices, on_device(): far = lax.ppermute(train, 'c', SWAP)  8.78 us
    ppermute x1, starting transfers between devices, on_device(): total = keep + lax.ppermute(send, 'z1', SWAP).astype(jnp.float32)  4.59 us
    all_to_all x1, starting transfers between devices, on_device(): plane = lax.all_to_all(eight, ('x', 'c'), 0, 0)  3.7 us
    ppermute x1, waiting for transfers between devices, on_device(): total = keep + lax.ppermute(send, 'z1', SWAP).astype(jnp.float32)  3.36 us
  transfers between devices with their start and end apart: 9, of which 4 were waited for; matrix products, arithmetic and copies ran while one was open for 0% of the time, Pallas kernels for 5%

profile of v6, /device:TPU:1, one launch (start us, length us, event | category | flops | bytes accessed | tf_op | source)
XLA Modules:
  0.0 127.4 jit_solution(18183932895948255193)
XLA Ops:
  0.0 8.8 %collective-permute-start = (bf16[512,2048]{1,0:T(8,128)(2,1)}, bf16[512,2048]{1,0:T(8,128)(2,1)}, u32[]{:S(2)}, u32[]{:S(2)}) collective-permute-start(bf16[512,2048]{1,0:T(8,128)(2,1)} %bitcast.14), channel_id=1, source_target_pairs={{0,1},{1,0},{2,3},{3,2},{4,5},{5,4},{6,7},{7,6},{8,9},{9,8},{10,11... | collective-permute-start | bytes 6291464 | tf_op jit(solution)/shard_map/ppermute | solution.py:126
  8.8 2.3 %spread.1 = bf16[8,64,2048]{2,1,0:T(8,128)(2,1)} custom-call(bf16[64,2048]{1,0:T(8,128)(2,1)} %bitcast.23), custom_call_target="tpu_custom_call" | custom-call | tf_op jit(solution)/shard_map/spread/pallas_call | solution.py:116
  11.1 0.0 copy-start.1
  11.1 3.7 %all-to-all-start = ((bf16[8,64,2048]{2,1,0:T(8,128)(2,1)}), bf16[8,64,2048]{2,1,0:T(8,128)(2,1)S(1)}, u32[]{:S(2)}, u32[]{:S(2)}) async-start(bf16[8,64,2048]{2,1,0:T(8,128)(2,1)} %spread.1), calls=%async_computation | async-start | bytes 4194304 | tf_op jit(solution)/shard_map/all_to_all | solution.py:124
  14.9 0.0 copy-done.1
  14.9 26.2 %all-gather = bf16[1,128,2048]{2,1,0:T(8,128)(2,1)S(1)} all-gather(bf16[1,32,2048]{2,1,0:T(8,128)(2,1)S(1)} %copy-done.1), channel_id=2, replica_groups=mesh['z1'=2,'z0'=2,'y'=4,'x'=4,'zh'=4,'c'=2] {'zh'}, dimensions={1}, use_global_device_ids=true | all-gather | bytes 655360 | tf_op jit(solution)/shard_map/all_gather | solution.py:127
  41.1 0.1 all-to-all-done
  41.2 0.0 copy-start
  41.2 0.7 condition.1
  41.9 25.8 %all_gather.7 = bf16[2,4,64,512]{3,2,1,0:T(8,128)(2,1)S(1)} all-gather(bf16[2,1,64,512]{3,2,1,0:T(8,128)(2,1)S(1)} %bitcast.22), channel_id=1, replica_groups=mesh['z1'=2,'z0'=2,'y'=4,'x'=4,'zh'=4,'c'=2] {'zh'}, dimensions={1}, use_global_device_ids=true | all-gather | bytes 655360 | tf_op jit(solution)/shard_map/all_gather | solution.py:137
  67.7 0.0 collective-permute-done.far_hbm
  67.8 2.5 %collective-permute-start.3 = (bf16[4,64,512]{2,1,0:T(8,128)(2,1)S(1)}, bf16[4,64,512]{2,1,0:T(8,128)(2,1)S(1)}, u32[]{:S(2)}, u32[]{:S(2)}) collective-permute-start(bf16[4,64,512]{2,1,0:T(8,128)(2,1)S(1)} %get-tuple-element.17.second_ref), channel_id=1, source_target_pairs={{0,24},{8,0},{16,8},{24,16},{1,25},{9,1},{17,9},{25,17},{2,26},{10... | collective-permute-start | bytes 786440 | tf_op jit(solution)/shard_map/ppermute | solution.py:44
  70.3 2.7 %collective-permute-start.1 = (bf16[4,64,512]{2,1,0:T(8,128)(2,1)S(1)}, bf16[4,64,512]{2,1,0:T(8,128)(2,1)S(1)}, u32[]{:S(2)}, u32[]{:S(2)}) collective-permute-start(bf16[4,64,512]{2,1,0:T(8,128)(2,1)S(1)} %get-tuple-element.18.first_ref), channel_id=1, source_target_pairs={{0,8},{8,16},{16,24},{24,0},{1,9},{9,17},{17,25},{25,1},{2,10},{10... | collective-permute-start | bytes 786440 | tf_op jit(solution)/shard_map/ppermute | solution.py:44
  73.1 2.0 %collective-permute-start.5 = (bf16[4,64,512]{2,1,0:T(8,128)(2,1)S(1)}, bf16[4,64,512]{2,1,0:T(8,128)(2,1)S(1)}, u32[]{:S(2)}, u32[]{:S(2)}) collective-permute-start(bf16[4,64,512]{2,1,0:T(8,128)(2,1)S(1)} %get-tuple-element.17.second_ref), channel_id=1, source_target_pairs={{0,8},{8,16},{16,24},{24,0},{1,9},{9,17},{17,25},{25,1},{2,10},{10... | collective-permute-start | bytes 786440 | tf_op jit(solution)/shard_map/ppermute | solution.py:44
  75.1 4.5 %collective-permute-start.6 = (bf16[4,64,512]{2,1,0:T(8,128)(2,1)S(1)}, bf16[4,64,512]{2,1,0:T(8,128)(2,1)S(1)}, u32[]{:S(2)}, u32[]{:S(2)}) collective-permute-start(bf16[4,64,512]{2,1,0:T(8,128)(2,1)S(1)} %get-tuple-element.18.first_ref), channel_id=1, source_target_pairs={{0,24},{8,0},{16,8},{24,16},{1,25},{9,1},{17,9},{25,17},{2,26},{10... | collective-permute-start | bytes 786440 | tf_op jit(solution)/shard_map/ppermute | solution.py:44
  79.6 0.0 collective-permute-done.3.refs_1_
  79.6 2.5 %collective-permute-start.4 = (bf16[4,64,512]{2,1,0:T(8,128)(2,1)S(1)}, bf16[4,64,512]{2,1,0:T(8,128)(2,1)S(1)}, u32[]{:S(2)}, u32[]{:S(2)}) collective-permute-start(bf16[4,64,512]{2,1,0:T(8,128)(2,1)S(1)} %collective-permute-done.3.refs_1_), channel_id=1, source_target_pairs={{0,24},{8,0},{16,8},{24,16},{1,25},{9,1},{17,9},{25,17},{2,26},{10... | collective-permute-start | bytes 786440 | tf_op jit(solution)/shard_map/ppermute | solution.py:44
  82.1 0.0 collective-permute-done.1.refs_0_
  82.1 2.7 %collective-permute-start.2 = (bf16[4,64,512]{2,1,0:T(8,128)(2,1)S(1)}, bf16[4,64,512]{2,1,0:T(8,128)(2,1)S(1)}, u32[]{:S(2)}, u32[]{:S(2)}) collective-permute-start(bf16[4,64,512]{2,1,0:T(8,128)(2,1)S(1)} %collective-permute-done.1.refs_0_), channel_id=1, source_target_pairs={{0,8},{8,16},{16,24},{24,0},{1,9},{9,17},{17,25},{25,1},{2,10},{10... | collective-permute-start | bytes 786440 | tf_op jit(solution)/shard_map/ppermute | solution.py:44
  84.9 0.0 copy-done
  84.9 2.4 %score_own.1 = (bf16[2,2,2,32,512]{4,3,2,1,0:T(8,128)(2,1)S(1)}, bf16[512,2048]{1,0:T(8,128)(2,1)S(1)}) custom-call(bf16[4,64,512]{2,1,0:T(8,128)(2,1)S(1)} %get-tuple-element.18.first_ref, bf16[4,64,512]{2,1,0:T(8,128)(2,1)S(1)} %get-tuple-element.17.second_ref, bf16[512,2048]{1,0:T(8,128)(2,1)S(1)} %bitcast.15, bf16[512,2048]{1,0:T(8,128)(2,1)} %collective-permute-done.far_hbm), custom_call_target="tpu_custom_call" | custom-call | flops 536870912 | bytes 6291456 | tf_op jit(solution)/shard_map/score_own/pallas_call | solution.py:152
  87.3 0.0 collective-permute-done.5.refs_2_
  87.3 0.0 collective-permute-done.6.refs_3_
  87.4 1.3 %score_sides.1.sides_ref = bf16[4,2,2,32,512]{4,3,2,1,0:T(8,128)(2,1)S(1)} custom-call(bf16[4,64,512]{2,1,0:T(8,128)(2,1)S(1)} %collective-permute-done.1.refs_0_, bf16[4,64,512]{2,1,0:T(8,128)(2,1)S(1)} %collective-permute-done.3.refs_1_, bf16[4,64,512]{2,1,0:T(8,128)(2,1)S(1)} %collective-permute-done.5.refs_2_, ...), custom_call_target="tpu_custom_call" | custom-call | flops 1073741824 | bytes 6291456 | tf_op jit(solution)/shard_map/score_sides/pallas_call | solution.py:163
  88.7 0.8 collective-permute-done.4.second_ref
  89.5 1.0 collective-permute-done.2.first_ref
  90.5 1.5 %score_last.1 = bf16[2,4,2,2,32,512]{5,4,3,2,1,0:T(8,128)(2,1)S(1)} custom-call(bf16[4,64,512]{2,1,0:T(8,128)(2,1)S(1)} %collective-permute-done.2.first_ref, bf16[4,64,512]{2,1,0:T(8,128)(2,1)S(1)} %collective-permute-done.4.second_ref, bf16[512,2048]{1,0:T(8,128)(2,1)S(1)} %bitcast.17, bf16[512,2048]{1,0:T(8,128)(2,1)S(1)} %get-tuple-element.13.refs_5_.far_ref, ...), custom_call_target="tpu_custom_call" | custom-call | flops 536870912 | bytes 6291456 | tf_op jit(solution)/shard_map/score_last/pallas_call | solution.py:169
  92.0 26.6 %all_to_all.10 = bf16[16,2,32,512]{3,2,1,0:T(8,128)(2,1)S(1)} all-to-all(bf16[16,2,32,512]{3,2,1,0:T(8,128)(2,1)S(1)} %bitcast.19), channel_id=1, replica_groups=mesh['z1'=2,'z0'=2,'y'=4,'x'=4,'zh'=4,'c'=2] {'z0','y','c'}, dimensions={0} | all-to-all | bytes 2097152 | tf_op jit(solution)/shard_map/all_to_all | solution.py:175
  118.6 0.1 sum_layers.1
  118.8 4.6 %collective-permute-start.7 = (bf16[2,32,512]{2,1,0:T(8,128)(2,1)S(1)}, bf16[2,32,512]{2,1,0:T(8,128)(2,1)S(1)}, u32[]{:S(2)}, u32[]{:S(2)}) collective-permute-start(bf16[2,32,512]{2,1,0:T(8,128)(2,1)S(1)} %get-tuple-element.16), channel_id=1, source_target_pairs={{0,256},{256,0},{1,257},{257,1},{2,258},{258,2},{3,259},{259,3},{4... | collective-permute-start | bytes 196616 | tf_op jit(solution)/shard_map/ppermute | solution.py:185
  123.4 3.4 %collective-permute-done.7 = bf16[2,32,512]{2,1,0:T(8,128)(2,1)S(1)} collective-permute-done((bf16[2,32,512]{2,1,0:T(8,128)(2,1)S(1)}, bf16[2,32,512]{2,1,0:T(8,128)(2,1)S(1)}, u32[]{:S(2)}, u32[]{:S(2)}) %collective-permute-start.7) | collective-permute-done | bytes 65568 | tf_op jit(solution)/shard_map/ppermute | solution.py:185
  126.7 0.7 convert_add_fusion
  (1 shorter events, 0.0 us)
Async XLA Ops:
  0.0 67.7 %collective-permute-start = (bf16[512,2048]{1,0:T(8,128)(2,1)}, bf16[512,2048]{1,0:T(8,128)(2,1)}, u32[]{:S(2)}, u32[]{:S(2)}) collective-permute-start(bf16[512,2048]{1,0:T(8,128)(2,1)} %bitcast.14), channel_id=1, source_target_pairs={{0,1},{1,0},{2,3},{3,2},{4,5},{5,4},{6,7},{7,6},{8,9},{9,8},{10,11... | collective-permute-start | bytes 6291464 | tf_op jit(solution)/shard_map/ppermute | solution.py:126
  11.1 3.7 %copy-start.1 = (bf16[1,32,2048]{2,1,0:T(8,128)(2,1)S(1)}, bf16[1,32,2048]{2,1,0:T(8,128)(2,1)}, u32[]{:S(2)}) copy-start(bf16[1,32,2048]{2,1,0:T(8,128)(2,1)} %param.4) | copy-start | bytes 393220
  11.1 30.0 %all-to-all-start = ((bf16[8,64,2048]{2,1,0:T(8,128)(2,1)}), bf16[8,64,2048]{2,1,0:T(8,128)(2,1)S(1)}, u32[]{:S(2)}, u32[]{:S(2)}) async-start(bf16[8,64,2048]{2,1,0:T(8,128)(2,1)} %spread.1), calls=%async_computation | async-start | bytes 4194304 | tf_op jit(solution)/shard_map/all_to_all | solution.py:124
  41.2 43.7 %copy-start = (bf16[1,512,2048]{2,1,0:T(8,128)(2,1)S(1)}, bf16[1,512,2048]{2,1,0:T(8,128)(2,1)}, u32[]{:S(2)}) copy-start(bf16[1,512,2048]{2,1,0:T(8,128)(2,1)} %param.3) | copy-start | bytes 6291460
  67.8 11.8 %collective-permute-start.3 = (bf16[4,64,512]{2,1,0:T(8,128)(2,1)S(1)}, bf16[4,64,512]{2,1,0:T(8,128)(2,1)S(1)}, u32[]{:S(2)}, u32[]{:S(2)}) collective-permute-start(bf16[4,64,512]{2,1,0:T(8,128)(2,1)S(1)} %get-tuple-element.17.second_ref), channel_id=1, source_target_pairs={{0,24},{8,0},{16,8},{24,16},{1,25},{9,1},{17,9},{25,17},{2,26},{10... | collective-permute-start | bytes 786440 | tf_op jit(solution)/shard_map/ppermute | solution.py:44
  70.3 11.8 %collective-permute-start.1 = (bf16[4,64,512]{2,1,0:T(8,128)(2,1)S(1)}, bf16[4,64,512]{2,1,0:T(8,128)(2,1)S(1)}, u32[]{:S(2)}, u32[]{:S(2)}) collective-permute-start(bf16[4,64,512]{2,1,0:T(8,128)(2,1)S(1)} %get-tuple-element.18.first_ref), channel_id=1, source_target_pairs={{0,8},{8,16},{16,24},{24,0},{1,9},{9,17},{17,25},{25,1},{2,10},{10... | collective-permute-start | bytes 786440 | tf_op jit(solution)/shard_map/ppermute | solution.py:44
  73.1 14.3 %collective-permute-start.5 = (bf16[4,64,512]{2,1,0:T(8,128)(2,1)S(1)}, bf16[4,64,512]{2,1,0:T(8,128)(2,1)S(1)}, u32[]{:S(2)}, u32[]{:S(2)}) collective-permute-start(bf16[4,64,512]{2,1,0:T(8,128)(2,1)S(1)} %get-tuple-element.17.second_ref), channel_id=1, source_target_pairs={{0,8},{8,16},{16,24},{24,0},{1,9},{9,17},{17,25},{25,1},{2,10},{10... | collective-permute-start | bytes 786440 | tf_op jit(solution)/shard_map/ppermute | solution.py:44
  75.1 12.3 %collective-permute-start.6 = (bf16[4,64,512]{2,1,0:T(8,128)(2,1)S(1)}, bf16[4,64,512]{2,1,0:T(8,128)(2,1)S(1)}, u32[]{:S(2)}, u32[]{:S(2)}) collective-permute-start(bf16[4,64,512]{2,1,0:T(8,128)(2,1)S(1)} %get-tuple-element.18.first_ref), channel_id=1, source_target_pairs={{0,24},{8,0},{16,8},{24,16},{1,25},{9,1},{17,9},{25,17},{2,26},{10... | collective-permute-start | bytes 786440 | tf_op jit(solution)/shard_map/ppermute | solution.py:44
  79.6 9.9 %collective-permute-start.4 = (bf16[4,64,512]{2,1,0:T(8,128)(2,1)S(1)}, bf16[4,64,512]{2,1,0:T(8,128)(2,1)S(1)}, u32[]{:S(2)}, u32[]{:S(2)}) collective-permute-start(bf16[4,64,512]{2,1,0:T(8,128)(2,1)S(1)} %collective-permute-done.3.refs_1_), channel_id=1, source_target_pairs={{0,24},{8,0},{16,8},{24,16},{1,25},{9,1},{17,9},{25,17},{2,26},{10... | collective-permute-start | bytes 786440 | tf_op jit(solution)/shard_map/ppermute | solution.py:44
  82.1 8.3 %collective-permute-start.2 = (bf16[4,64,512]{2,1,0:T(8,128)(2,1)S(1)}, bf16[4,64,512]{2,1,0:T(8,128)(2,1)S(1)}, u32[]{:S(2)}, u32[]{:S(2)}) collective-permute-start(bf16[4,64,512]{2,1,0:T(8,128)(2,1)S(1)} %collective-permute-done.1.refs_0_), channel_id=1, source_target_pairs={{0,8},{8,16},{16,24},{24,0},{1,9},{9,17},{17,25},{25,1},{2,10},{10... | collective-permute-start | bytes 786440 | tf_op jit(solution)/shard_map/ppermute | solution.py:44
  118.8 8.0 %collective-permute-start.7 = (bf16[2,32,512]{2,1,0:T(8,128)(2,1)S(1)}, bf16[2,32,512]{2,1,0:T(8,128)(2,1)S(1)}, u32[]{:S(2)}, u32[]{:S(2)}) collective-permute-start(bf16[2,32,512]{2,1,0:T(8,128)(2,1)S(1)} %get-tuple-element.16), channel_id=1, source_target_pairs={{0,256},{256,0},{1,257},{257,1},{2,258},{258,2},{3,259},{259,3},{4... | collective-permute-start | bytes 196616 | tf_op jit(solution)/shard_map/ppermute | solution.py:185

commit v7 on v6

--- a/solution.py
+++ b/solution.py
@@ -89,12 +89,12 @@
     for order, scored in ((OWN, own_ref), (SIDES, sides_ref)):
         for n, (step, half) in enumerate(order):
             at = lax.rem(x + step, 4)
-            out_ref[lax.rem(at, 2), 2 * half : 2 * half + 2, :, at // 2] = scored[n]
+            out_ref[2 * half : 2 * half + 2, :, lax.rem(at, 2), at // 2] = scored[n]
 
     def put(owner, at, block):
         to = lax.rem(x + 2, 4)
         for n, (_, half) in enumerate(OPPOSITE):
-            out_ref[lax.rem(to, 2), 2 * half : 2 * half + 2, owner, to // 2, :, at : at + 256] = block[n]
+            out_ref[2 * half : 2 * half + 2, owner, lax.rem(to, 2), to // 2, :, at : at + 256] = block[n]
 
     score((first_ref, second_ref), (near_ref, far_ref), put)
 
@@ -103,9 +103,9 @@
     mine = lax.axis_index("z1")
     for side in range(2):
         for out_ref, z1 in ((keep_ref, mine), (send_ref, 1 - mine)):
-            total = part_ref[0, side, z1].astype(jnp.float32)
-            for n in range(1, 8):
-                total += part_ref[n, side, z1].astype(jnp.float32)
+            total = jnp.zeros(keep_ref.shape[1:], jnp.float32)
+            for n in range(8):
+                total += part_ref[n // 2, side, n % 2, z1].astype(jnp.float32)
             out_ref[side] = total.astype(out_ref.dtype)
 
 
@@ -168,11 +168,11 @@
     )(behind_first, ahead_second, behind_second, ahead_first, train, far)
     part = pl.pallas_call(
         score_last,
-        out_shape=jax.ShapeDtypeStruct((2, 4, 2, 2, mine, rows), jnp.bfloat16),
+        out_shape=jax.ShapeDtypeStruct((4, 2, 2, 2, mine, rows), jnp.bfloat16),
         name="score_last",
         **options(2),
     )(opposite_first, opposite_second, train, far, own, sides)
-    part = lax.all_to_all(part.reshape(16, 2, mine, rows), ("z0", "y", "c"), 0, 0)
+    part = lax.all_to_all(part.reshape(16, 2, mine, rows), ("y", "c", "z0"), 0, 0)
     keep, send = pl.pallas_call(
         sum_layers,
         out_shape=(
@@ -181,7 +181,7 @@
         ),
         compiler_params=pltpu.CompilerParams(vmem_limit_bytes=14 * 2**20),
         name="sum_layers",
-    )(part.reshape(8, 2, 2, mine, rows))
+    )(part.reshape(4, 2, 2, 2, mine, rows))
     total = keep + lax.ppermute(send, "z1", SWAP).astype(jnp.float32)
     return total.reshape(2 * mine, rows).T
 

time: 128 us -> 127 us (level)
  no operation moved by 1% of the time
where the time goes in v7:
time: 127 us; the launch traced here: 126 us
  blocking collectives  78.6 us (62%)
  starting transfers between devices  34.1 us (27%)
  Pallas kernels  8.41 us (7%)
  waiting for transfers between devices  4.08 us (3%)
    all_to_all x1, blocking collectives, on_device(): lax.all_to_all(part.reshape(16, 2, mine, rows), ('y', 'c', 'z0'), 0, 0)  26.5 us
    all_gather x1, blocking collectives, on_device(): queries = lax.all_gather(query, 'zh', axis=0, tiled=True)  26.2 us
    all_gather x1, blocking collectives, on_device(): lax.all_gather(conditioned.reshape(2, 2 * mine, -1), 'zh', axis=1)  25.8 us
    ppermute x6, starting transfers between devices, shift_x(): return lax.ppermute(block, 'x', [(i, (i + by) % 4) for i in range(4)])  17.1 us
    ppermute x1, starting transfers between devices, on_device(): far = lax.ppermute(train, 'c', SWAP)  8.78 us
    ppermute x1, starting transfers between devices, on_device(): total = keep + lax.ppermute(send, 'z1', SWAP).astype(jnp.float32)  4.59 us
    all_to_all x1, starting transfers between devices, on_device(): plane = lax.all_to_all(eight, ('x', 'c'), 0, 0)  3.7 us
  transfers between devices with their start and end apart: 9, of which 4 were waited for; matrix products, arithmetic and copies ran while one was open for 0% of the time, Pallas kernels for 5%

profile of v7, /device:TPU:1, one launch (start us, length us, event | category | flops | bytes accessed | tf_op | source)
XLA Modules:
  0.0 126.1 jit_solution(10904748264568058677)
XLA Ops:
  0.0 8.8 %collective-permute-start = (bf16[512,2048]{1,0:T(8,128)(2,1)}, bf16[512,2048]{1,0:T(8,128)(2,1)}, u32[]{:S(2)}, u32[]{:S(2)}) collective-permute-start(bf16[512,2048]{1,0:T(8,128)(2,1)} %bitcast.14), channel_id=1, source_target_pairs={{0,1},{1,0},{2,3},{3,2},{4,5},{5,4},{6,7},{7,6},{8,9},{9,8},{10,11... | collective-permute-start | bytes 6291464 | tf_op jit(solution)/shard_map/ppermute | solution.py:126
  8.8 2.3 %spread.1 = bf16[8,64,2048]{2,1,0:T(8,128)(2,1)} custom-call(bf16[64,2048]{1,0:T(8,128)(2,1)} %bitcast.23), custom_call_target="tpu_custom_call" | custom-call | tf_op jit(solution)/shard_map/spread/pallas_call | solution.py:116
  11.1 0.0 copy-start.1
  11.1 3.7 %all-to-all-start = ((bf16[8,64,2048]{2,1,0:T(8,128)(2,1)}), bf16[8,64,2048]{2,1,0:T(8,128)(2,1)S(1)}, u32[]{:S(2)}, u32[]{:S(2)}) async-start(bf16[8,64,2048]{2,1,0:T(8,128)(2,1)} %spread.1), calls=%async_computation | async-start | bytes 4194304 | tf_op jit(solution)/shard_map/all_to_all | solution.py:124
  14.9 0.0 copy-done.1
  14.9 26.2 %all-gather = bf16[1,128,2048]{2,1,0:T(8,128)(2,1)S(1)} all-gather(bf16[1,32,2048]{2,1,0:T(8,128)(2,1)S(1)} %copy-done.1), channel_id=2, replica_groups=mesh['z1'=2,'z0'=2,'y'=4,'x'=4,'zh'=4,'c'=2] {'zh'}, dimensions={1}, use_global_device_ids=true | all-gather | bytes 655360 | tf_op jit(solution)/shard_map/all_gather | solution.py:127
  41.1 0.1 all-to-all-done
  41.2 0.0 copy-start
  41.2 0.7 condition.1
  41.9 25.8 %all_gather.7 = bf16[2,4,64,512]{3,2,1,0:T(8,128)(2,1)S(1)} all-gather(bf16[2,1,64,512]{3,2,1,0:T(8,128)(2,1)S(1)} %bitcast.22), channel_id=1, replica_groups=mesh['z1'=2,'z0'=2,'y'=4,'x'=4,'zh'=4,'c'=2] {'zh'}, dimensions={1}, use_global_device_ids=true | all-gather | bytes 655360 | tf_op jit(solution)/shard_map/all_gather | solution.py:137
  67.7 0.0 collective-permute-done.far_hbm
  67.8 2.5 %collective-permute-start.3 = (bf16[4,64,512]{2,1,0:T(8,128)(2,1)S(1)}, bf16[4,64,512]{2,1,0:T(8,128)(2,1)S(1)}, u32[]{:S(2)}, u32[]{:S(2)}) collective-permute-start(bf16[4,64,512]{2,1,0:T(8,128)(2,1)S(1)} %get-tuple-element.17.second_ref), channel_id=1, source_target_pairs={{0,24},{8,0},{16,8},{24,16},{1,25},{9,1},{17,9},{25,17},{2,26},{10... | collective-permute-start | bytes 786440 | tf_op jit(solution)/shard_map/ppermute | solution.py:44
  70.3 2.7 %collective-permute-start.1 = (bf16[4,64,512]{2,1,0:T(8,128)(2,1)S(1)}, bf16[4,64,512]{2,1,0:T(8,128)(2,1)S(1)}, u32[]{:S(2)}, u32[]{:S(2)}) collective-permute-start(bf16[4,64,512]{2,1,0:T(8,128)(2,1)S(1)} %get-tuple-element.18.first_ref), channel_id=1, source_target_pairs={{0,8},{8,16},{16,24},{24,0},{1,9},{9,17},{17,25},{25,1},{2,10},{10... | collective-permute-start | bytes 786440 | tf_op jit(solution)/shard_map/ppermute | solution.py:44
  73.1 2.0 %collective-permute-start.5 = (bf16[4,64,512]{2,1,0:T(8,128)(2,1)S(1)}, bf16[4,64,512]{2,1,0:T(8,128)(2,1)S(1)}, u32[]{:S(2)}, u32[]{:S(2)}) collective-permute-start(bf16[4,64,512]{2,1,0:T(8,128)(2,1)S(1)} %get-tuple-element.17.second_ref), channel_id=1, source_target_pairs={{0,8},{8,16},{16,24},{24,0},{1,9},{9,17},{17,25},{25,1},{2,10},{10... | collective-permute-start | bytes 786440 | tf_op jit(solution)/shard_map/ppermute | solution.py:44
  75.1 4.5 %collective-permute-start.6 = (bf16[4,64,512]{2,1,0:T(8,128)(2,1)S(1)}, bf16[4,64,512]{2,1,0:T(8,128)(2,1)S(1)}, u32[]{:S(2)}, u32[]{:S(2)}) collective-permute-start(bf16[4,64,512]{2,1,0:T(8,128)(2,1)S(1)} %get-tuple-element.18.first_ref), channel_id=1, source_target_pairs={{0,24},{8,0},{16,8},{24,16},{1,25},{9,1},{17,9},{25,17},{2,26},{10... | collective-permute-start | bytes 786440 | tf_op jit(solution)/shard_map/ppermute | solution.py:44
  79.6 0.0 collective-permute-done.3.refs_1_
  79.6 2.5 %collective-permute-start.4 = (bf16[4,64,512]{2,1,0:T(8,128)(2,1)S(1)}, bf16[4,64,512]{2,1,0:T(8,128)(2,1)S(1)}, u32[]{:S(2)}, u32[]{:S(2)}) collective-permute-start(bf16[4,64,512]{2,1,0:T(8,128)(2,1)S(1)} %collective-permute-done.3.refs_1_), channel_id=1, source_target_pairs={{0,24},{8,0},{16,8},{24,16},{1,25},{9,1},{17,9},{25,17},{2,26},{10... | collective-permute-start | bytes 786440 | tf_op jit(solution)/shard_map/ppermute | solution.py:44
  82.1 0.0 collective-permute-done.1.refs_0_
  82.1 2.7 %collective-permute-start.2 = (bf16[4,64,512]{2,1,0:T(8,128)(2,1)S(1)}, bf16[4,64,512]{2,1,0:T(8,128)(2,1)S(1)}, u32[]{:S(2)}, u32[]{:S(2)}) collective-permute-start(bf16[4,64,512]{2,1,0:T(8,128)(2,1)S(1)} %collective-permute-done.1.refs_0_), channel_id=1, source_target_pairs={{0,8},{8,16},{16,24},{24,0},{1,9},{9,17},{17,25},{25,1},{2,10},{10... | collective-permute-start | bytes 786440 | tf_op jit(solution)/shard_map/ppermute | solution.py:44
  84.9 0.0 copy-done
  84.9 2.4 %score_own.1 = (bf16[2,2,2,32,512]{4,3,2,1,0:T(8,128)(2,1)S(1)}, bf16[512,2048]{1,0:T(8,128)(2,1)S(1)}) custom-call(bf16[4,64,512]{2,1,0:T(8,128)(2,1)S(1)} %get-tuple-element.18.first_ref, bf16[4,64,512]{2,1,0:T(8,128)(2,1)S(1)} %get-tuple-element.17.second_ref, bf16[512,2048]{1,0:T(8,128)(2,1)S(1)} %bitcast.15, bf16[512,2048]{1,0:T(8,128)(2,1)} %collective-permute-done.far_hbm), custom_call_target="tpu_custom_call" | custom-call | flops 536870912 | bytes 6291456 | tf_op jit(solution)/shard_map/score_own/pallas_call | solution.py:152
  87.3 0.0 collective-permute-done.5.refs_2_
  87.3 0.0 collective-permute-done.6.refs_3_
  87.4 1.3 %score_sides.1.sides_ref = bf16[4,2,2,32,512]{4,3,2,1,0:T(8,128)(2,1)S(1)} custom-call(bf16[4,64,512]{2,1,0:T(8,128)(2,1)S(1)} %collective-permute-done.1.refs_0_, bf16[4,64,512]{2,1,0:T(8,128)(2,1)S(1)} %collective-permute-done.3.refs_1_, bf16[4,64,512]{2,1,0:T(8,128)(2,1)S(1)} %collective-permute-done.5.refs_2_, ...), custom_call_target="tpu_custom_call" | custom-call | flops 1073741824 | bytes 6291456 | tf_op jit(solution)/shard_map/score_sides/pallas_call | solution.py:163
  88.7 0.8 collective-permute-done.4.second_ref
  89.5 1.0 collective-permute-done.2.first_ref
  90.5 1.5 %score_last.1 = bf16[4,2,2,2,32,512]{5,4,3,2,1,0:T(8,128)(2,1)S(1)} custom-call(bf16[4,64,512]{2,1,0:T(8,128)(2,1)S(1)} %collective-permute-done.2.first_ref, bf16[4,64,512]{2,1,0:T(8,128)(2,1)S(1)} %collective-permute-done.4.second_ref, bf16[512,2048]{1,0:T(8,128)(2,1)S(1)} %bitcast.17, bf16[512,2048]{1,0:T(8,128)(2,1)S(1)} %get-tuple-element.13.refs_5_.far_ref, ...), custom_call_target="tpu_custom_call" | custom-call | flops 536870912 | bytes 6291456 | tf_op jit(solution)/shard_map/score_last/pallas_call | solution.py:169
  92.0 26.5 %all_to_all.10 = bf16[16,2,32,512]{3,2,1,0:T(8,128)(2,1)S(1)} all-to-all(bf16[16,2,32,512]{3,2,1,0:T(8,128)(2,1)S(1)} %bitcast.19), channel_id=1, replica_groups=mesh['z1'=2,'z0'=2,'y'=4,'x'=4,'zh'=4,'c'=2] {'y','c','z0'}, dimensions={0} | all-to-all | bytes 2097152 | tf_op jit(solution)/shard_map/all_to_all | solution.py:175
  118.5 0.1 sum_layers.1
  118.6 4.6 %collective-permute-start.7 = (bf16[2,32,512]{2,1,0:T(8,128)(2,1)S(1)}, bf16[2,32,512]{2,1,0:T(8,128)(2,1)S(1)}, u32[]{:S(2)}, u32[]{:S(2)}) collective-permute-start(bf16[2,32,512]{2,1,0:T(8,128)(2,1)S(1)} %get-tuple-element.16), channel_id=1, source_target_pairs={{0,256},{256,0},{1,257},{257,1},{2,258},{258,2},{3,259},{259,3},{4... | collective-permute-start | bytes 196616 | tf_op jit(solution)/shard_map/ppermute | solution.py:185
  123.2 2.2 %collective-permute-done.7 = bf16[2,32,512]{2,1,0:T(8,128)(2,1)S(1)} collective-permute-done((bf16[2,32,512]{2,1,0:T(8,128)(2,1)S(1)}, bf16[2,32,512]{2,1,0:T(8,128)(2,1)S(1)}, u32[]{:S(2)}, u32[]{:S(2)}) %collective-permute-start.7) | collective-permute-done | bytes 65568 | tf_op jit(solution)/shard_map/ppermute | solution.py:185
  125.4 0.7 convert_add_fusion
  (1 shorter events, 0.0 us)
Async XLA Ops:
  0.0 67.7 %collective-permute-start = (bf16[512,2048]{1,0:T(8,128)(2,1)}, bf16[512,2048]{1,0:T(8,128)(2,1)}, u32[]{:S(2)}, u32[]{:S(2)}) collective-permute-start(bf16[512,2048]{1,0:T(8,128)(2,1)} %bitcast.14), channel_id=1, source_target_pairs={{0,1},{1,0},{2,3},{3,2},{4,5},{5,4},{6,7},{7,6},{8,9},{9,8},{10,11... | collective-permute-start | bytes 6291464 | tf_op jit(solution)/shard_map/ppermute | solution.py:126
  11.1 3.7 %copy-start.1 = (bf16[1,32,2048]{2,1,0:T(8,128)(2,1)S(1)}, bf16[1,32,2048]{2,1,0:T(8,128)(2,1)}, u32[]{:S(2)}) copy-start(bf16[1,32,2048]{2,1,0:T(8,128)(2,1)} %param.4) | copy-start | bytes 393220
  11.1 30.0 %all-to-all-start = ((bf16[8,64,2048]{2,1,0:T(8,128)(2,1)}), bf16[8,64,2048]{2,1,0:T(8,128)(2,1)S(1)}, u32[]{:S(2)}, u32[]{:S(2)}) async-start(bf16[8,64,2048]{2,1,0:T(8,128)(2,1)} %spread.1), calls=%async_computation | async-start | bytes 4194304 | tf_op jit(solution)/shard_map/all_to_all | solution.py:124
  41.2 43.7 %copy-start = (bf16[1,512,2048]{2,1,0:T(8,128)(2,1)S(1)}, bf16[1,512,2048]{2,1,0:T(8,128)(2,1)}, u32[]{:S(2)}) copy-start(bf16[1,512,2048]{2,1,0:T(8,128)(2,1)} %param.3) | copy-start | bytes 6291460
  67.8 11.8 %collective-permute-start.3 = (bf16[4,64,512]{2,1,0:T(8,128)(2,1)S(1)}, bf16[4,64,512]{2,1,0:T(8,128)(2,1)S(1)}, u32[]{:S(2)}, u32[]{:S(2)}) collective-permute-start(bf16[4,64,512]{2,1,0:T(8,128)(2,1)S(1)} %get-tuple-element.17.second_ref), channel_id=1, source_target_pairs={{0,24},{8,0},{16,8},{24,16},{1,25},{9,1},{17,9},{25,17},{2,26},{10... | collective-permute-start | bytes 786440 | tf_op jit(solution)/shard_map/ppermute | solution.py:44
  70.3 11.8 %collective-permute-start.1 = (bf16[4,64,512]{2,1,0:T(8,128)(2,1)S(1)}, bf16[4,64,512]{2,1,0:T(8,128)(2,1)S(1)}, u32[]{:S(2)}, u32[]{:S(2)}) collective-permute-start(bf16[4,64,512]{2,1,0:T(8,128)(2,1)S(1)} %get-tuple-element.18.first_ref), channel_id=1, source_target_pairs={{0,8},{8,16},{16,24},{24,0},{1,9},{9,17},{17,25},{25,1},{2,10},{10... | collective-permute-start | bytes 786440 | tf_op jit(solution)/shard_map/ppermute | solution.py:44
  73.1 14.3 %collective-permute-start.5 = (bf16[4,64,512]{2,1,0:T(8,128)(2,1)S(1)}, bf16[4,64,512]{2,1,0:T(8,128)(2,1)S(1)}, u32[]{:S(2)}, u32[]{:S(2)}) collective-permute-start(bf16[4,64,512]{2,1,0:T(8,128)(2,1)S(1)} %get-tuple-element.17.second_ref), channel_id=1, source_target_pairs={{0,8},{8,16},{16,24},{24,0},{1,9},{9,17},{17,25},{25,1},{2,10},{10... | collective-permute-start | bytes 786440 | tf_op jit(solution)/shard_map/ppermute | solution.py:44
  75.1 12.3 %collective-permute-start.6 = (bf16[4,64,512]{2,1,0:T(8,128)(2,1)S(1)}, bf16[4,64,512]{2,1,0:T(8,128)(2,1)S(1)}, u32[]{:S(2)}, u32[]{:S(2)}) collective-permute-start(bf16[4,64,512]{2,1,0:T(8,128)(2,1)S(1)} %get-tuple-element.18.first_ref), channel_id=1, source_target_pairs={{0,24},{8,0},{16,8},{24,16},{1,25},{9,1},{17,9},{25,17},{2,26},{10... | collective-permute-start | bytes 786440 | tf_op jit(solution)/shard_map/ppermute | solution.py:44
  79.6 9.9 %collective-permute-start.4 = (bf16[4,64,512]{2,1,0:T(8,128)(2,1)S(1)}, bf16[4,64,512]{2,1,0:T(8,128)(2,1)S(1)}, u32[]{:S(2)}, u32[]{:S(2)}) collective-permute-start(bf16[4,64,512]{2,1,0:T(8,128)(2,1)S(1)} %collective-permute-done.3.refs_1_), channel_id=1, source_target_pairs={{0,24},{8,0},{16,8},{24,16},{1,25},{9,1},{17,9},{25,17},{2,26},{10... | collective-permute-start | bytes 786440 | tf_op jit(solution)/shard_map/ppermute | solution.py:44
  82.1 8.3 %collective-permute-start.2 = (bf16[4,64,512]{2,1,0:T(8,128)(2,1)S(1)}, bf16[4,64,512]{2,1,0:T(8,128)(2,1)S(1)}, u32[]{:S(2)}, u32[]{:S(2)}) collective-permute-start(bf16[4,64,512]{2,1,0:T(8,128)(2,1)S(1)} %collective-permute-done.1.refs_0_), channel_id=1, source_target_pairs={{0,8},{8,16},{16,24},{24,0},{1,9},{9,17},{17,25},{25,1},{2,10},{10... | collective-permute-start | bytes 786440 | tf_op jit(solution)/shard_map/ppermute | solution.py:44
  118.6 6.8 %collective-permute-start.7 = (bf16[2,32,512]{2,1,0:T(8,128)(2,1)S(1)}, bf16[2,32,512]{2,1,0:T(8,128)(2,1)S(1)}, u32[]{:S(2)}, u32[]{:S(2)}) collective-permute-start(bf16[2,32,512]{2,1,0:T(8,128)(2,1)S(1)} %get-tuple-element.16), channel_id=1, source_target_pairs={{0,256},{256,0},{1,257},{257,1},{2,258},{258,2},{3,259},{259,3},{4... | collective-permute-start | bytes 196616 | tf_op jit(solution)/shard_map/ppermute | solution.py:185

commit v8 on v7

--- a/solution.py
+++ b/solution.py
@@ -13,14 +13,6 @@
 
 def copies(block, n):
     return jnp.broadcast_to(block[None], (n,) + block.shape)
-
-
-def spread(block_ref, out_ref, sem):
-    sent = [pltpu.make_async_copy(block_ref, out_ref.at[n], sem.at[n]) for n in range(8)]
-    for copy in sent:
-        copy.start()
-    for copy in sent:
-        copy.wait()
 
 
 def rows_by_rows(a, b):
@@ -113,15 +105,7 @@
     train, query, fisher = train_grads[0], query_grads[0], inverse_fisher[0]
     rows, k = train.shape
     mine = query.shape[0]
-    eight = pl.pallas_call(
-        spread,
-        out_shape=jax.ShapeDtypeStruct((8,) + fisher.shape, fisher.dtype),
-        in_specs=[pl.BlockSpec(memory_space=pltpu.VMEM)],
-        out_specs=pl.BlockSpec(memory_space=pl.ANY),
-        scratch_shapes=[pltpu.SemaphoreType.DMA((8,))],
-        name="spread",
-    )(fisher)
-    plane = lax.all_to_all(eight, ("x", "c"), 0, 0)
+    plane = lax.all_to_all(copies(fisher, 8), ("x", "c"), 0, 0)
     plane = plane.reshape(4, -1, k)
     far = lax.ppermute(train, "c", SWAP)
     queries = lax.all_gather(query, "zh", axis=0, tiled=True)

time: 127 us -> 126 us (level)
  local copies, waits for them, and re-layouts: 0.04 us -> 2.57 us
  Pallas kernels: 8.41 us -> 6.07 us
    broadcast_in_dim x0 -> x1, local copies, waits for them, and re-layouts: none -> 2.53 us  [copies(): return jnp.broadcast_to(block[None], (n,) + block.shape)]
    pallas_call x1 -> x0, Pallas kernels: 2.34 us -> none  [on_device(): pl.pallas_call(spread, out_shape=jax.ShapeDtypeStruct((8,) + fisher.shape...]
  transfers between devices with their start and end apart: 9 -> 9, of which waited for: 4 -> 4; matrix products, arithmetic and copies ran while one was open for 0% -> 2% of each run, Pallas kernels for 5% -> 4%
where the time goes in v8:
time: 126 us; the launch traced here: 125 us
  blocking collectives  78.1 us (62%)
  starting transfers between devices  32.9 us (26%)
  Pallas kernels  6.07 us (5%)
  waiting for transfers between devices  4.25 us (3%)
  local copies, waits for them, and re-layouts  2.57 us (2%)
    all_gather x1, blocking collectives, on_device(): queries = lax.all_gather(query, 'zh', axis=0, tiled=True)  26.2 us
    all_to_all x1, blocking collectives, on_device(): lax.all_to_all(part.reshape(16, 2, mine, rows), ('y', 'c', 'z0'), 0, 0)  26 us
    all_gather x1, blocking collectives, on_device(): lax.all_gather(conditioned.reshape(2, 2 * mine, -1), 'zh', axis=1)  25.9 us
    ppermute x6, starting transfers between devices, shift_x(): return lax.ppermute(block, 'x', [(i, (i + by) % 4) for i in range(4)])  17.1 us
    ppermute x1, starting transfers between devices, on_device(): far = lax.ppermute(train, 'c', SWAP)  8.78 us
    all_to_all x1, starting transfers between devices, on_device(): plane = lax.all_to_all(copies(fisher, 8), ('x', 'c'), 0, 0)  3.68 us
    ppermute x1, starting transfers between devices, on_device(): total = keep + lax.ppermute(send, 'z1', SWAP).astype(jnp.float32)  3.43 us
    broadcast_in_dim x1, local copies, waits for them, and re-layouts, copies(): return jnp.broadcast_to(block[None], (n,) + block.shape)  2.53 us
  transfers between devices with their start and end apart: 9, of which 4 were waited for; matrix products, arithmetic and copies ran while one was open for 2% of the time, Pallas kernels for 4%

profile of v8, /device:TPU:1, one launch (start us, length us, event | category | flops | bytes accessed | tf_op | source)
XLA Modules:
  0.0 124.7 jit_solution(8674536195560350868)
XLA Ops:
  0.0 8.8 %collective-permute-start = (bf16[512,2048]{1,0:T(8,128)(2,1)}, bf16[512,2048]{1,0:T(8,128)(2,1)}, u32[]{:S(2)}, u32[]{:S(2)}) collective-permute-start(bf16[512,2048]{1,0:T(8,128)(2,1)} %bitcast.14), channel_id=1, source_target_pairs={{0,1},{1,0},{2,3},{3,2},{4,5},{5,4},{6,7},{7,6},{8,9},{9,8},{10,11... | collective-permute-start | bytes 6291464 | tf_op jit(solution)/shard_map/ppermute | solution.py:110
  8.8 2.5 %broadcast_in_dim.8 = bf16[8,64,2048]{2,1,0:T(8,128)(2,1)} broadcast(bf16[64,2048]{1,0:T(8,128)(2,1)} %bitcast.23), dimensions={1,2} | broadcast | bytes 2359296 | tf_op jit(solution)/shard_map/broadcast_in_dim | solution.py:15
  11.3 0.0 copy-start.1
  11.3 3.7 %all-to-all-start = ((bf16[8,64,2048]{2,1,0:T(8,128)(2,1)}), bf16[8,64,2048]{2,1,0:T(8,128)(2,1)S(1)}, u32[]{:S(2)}, u32[]{:S(2)}) async-start(bf16[8,64,2048]{2,1,0:T(8,128)(2,1)} %broadcast_in_dim.8), calls=%async_computation | async-start | bytes 4194304 | tf_op jit(solution)/shard_map/all_to_all | solution.py:108
  15.0 0.0 copy-done.1
  15.0 26.2 %all-gather = bf16[1,128,2048]{2,1,0:T(8,128)(2,1)S(1)} all-gather(bf16[1,32,2048]{2,1,0:T(8,128)(2,1)S(1)} %copy-done.1), channel_id=2, replica_groups=mesh['z1'=2,'z0'=2,'y'=4,'x'=4,'zh'=4,'c'=2] {'zh'}, dimensions={1}, use_global_device_ids=true | all-gather | bytes 655360 | tf_op jit(solution)/shard_map/all_gather | solution.py:111
  41.3 0.1 all-to-all-done
  41.3 0.0 copy-start
  41.3 0.7 condition.1
  42.0 25.9 %all_gather.7 = bf16[2,4,64,512]{3,2,1,0:T(8,128)(2,1)S(1)} all-gather(bf16[2,1,64,512]{3,2,1,0:T(8,128)(2,1)S(1)} %bitcast.22), channel_id=1, replica_groups=mesh['z1'=2,'z0'=2,'y'=4,'x'=4,'zh'=4,'c'=2] {'zh'}, dimensions={1}, use_global_device_ids=true | all-gather | bytes 655360 | tf_op jit(solution)/shard_map/all_gather | solution.py:121
  67.9 0.0 collective-permute-done.far_hbm
  67.9 2.4 %collective-permute-start.3 = (bf16[4,64,512]{2,1,0:T(8,128)(2,1)S(1)}, bf16[4,64,512]{2,1,0:T(8,128)(2,1)S(1)}, u32[]{:S(2)}, u32[]{:S(2)}) collective-permute-start(bf16[4,64,512]{2,1,0:T(8,128)(2,1)S(1)} %get-tuple-element.17.second_ref), channel_id=1, source_target_pairs={{0,24},{8,0},{16,8},{24,16},{1,25},{9,1},{17,9},{25,17},{2,26},{10... | collective-permute-start | bytes 786440 | tf_op jit(solution)/shard_map/ppermute | solution.py:36
  70.4 2.9 %collective-permute-start.1 = (bf16[4,64,512]{2,1,0:T(8,128)(2,1)S(1)}, bf16[4,64,512]{2,1,0:T(8,128)(2,1)S(1)}, u32[]{:S(2)}, u32[]{:S(2)}) collective-permute-start(bf16[4,64,512]{2,1,0:T(8,128)(2,1)S(1)} %get-tuple-element.18.first_ref), channel_id=1, source_target_pairs={{0,8},{8,16},{16,24},{24,0},{1,9},{9,17},{17,25},{25,1},{2,10},{10... | collective-permute-start | bytes 786440 | tf_op jit(solution)/shard_map/ppermute | solution.py:36
  73.2 2.0 %collective-permute-start.5 = (bf16[4,64,512]{2,1,0:T(8,128)(2,1)S(1)}, bf16[4,64,512]{2,1,0:T(8,128)(2,1)S(1)}, u32[]{:S(2)}, u32[]{:S(2)}) collective-permute-start(bf16[4,64,512]{2,1,0:T(8,128)(2,1)S(1)} %get-tuple-element.17.second_ref), channel_id=1, source_target_pairs={{0,8},{8,16},{16,24},{24,0},{1,9},{9,17},{17,25},{25,1},{2,10},{10... | collective-permute-start | bytes 786440 | tf_op jit(solution)/shard_map/ppermute | solution.py:36
  75.2 4.5 %collective-permute-start.6 = (bf16[4,64,512]{2,1,0:T(8,128)(2,1)S(1)}, bf16[4,64,512]{2,1,0:T(8,128)(2,1)S(1)}, u32[]{:S(2)}, u32[]{:S(2)}) collective-permute-start(bf16[4,64,512]{2,1,0:T(8,128)(2,1)S(1)} %get-tuple-element.18.first_ref), channel_id=1, source_target_pairs={{0,24},{8,0},{16,8},{24,16},{1,25},{9,1},{17,9},{25,17},{2,26},{10... | collective-permute-start | bytes 786440 | tf_op jit(solution)/shard_map/ppermute | solution.py:36
  79.7 0.0 collective-permute-done.3.refs_1_
  79.7 2.4 %collective-permute-start.4 = (bf16[4,64,512]{2,1,0:T(8,128)(2,1)S(1)}, bf16[4,64,512]{2,1,0:T(8,128)(2,1)S(1)}, u32[]{:S(2)}, u32[]{:S(2)}) collective-permute-start(bf16[4,64,512]{2,1,0:T(8,128)(2,1)S(1)} %collective-permute-done.3.refs_1_), channel_id=1, source_target_pairs={{0,24},{8,0},{16,8},{24,16},{1,25},{9,1},{17,9},{25,17},{2,26},{10... | collective-permute-start | bytes 786440 | tf_op jit(solution)/shard_map/ppermute | solution.py:36
  82.2 0.0 collective-permute-done.1.refs_0_
  82.2 2.8 %collective-permute-start.2 = (bf16[4,64,512]{2,1,0:T(8,128)(2,1)S(1)}, bf16[4,64,512]{2,1,0:T(8,128)(2,1)S(1)}, u32[]{:S(2)}, u32[]{:S(2)}) collective-permute-start(bf16[4,64,512]{2,1,0:T(8,128)(2,1)S(1)} %collective-permute-done.1.refs_0_), channel_id=1, source_target_pairs={{0,8},{8,16},{16,24},{24,0},{1,9},{9,17},{17,25},{25,1},{2,10},{10... | collective-permute-start | bytes 786440 | tf_op jit(solution)/shard_map/ppermute | solution.py:36
  85.1 0.0 copy-done
  85.1 2.4 %score_own.1 = (bf16[2,2,2,32,512]{4,3,2,1,0:T(8,128)(2,1)S(1)}, bf16[512,2048]{1,0:T(8,128)(2,1)S(1)}) custom-call(bf16[4,64,512]{2,1,0:T(8,128)(2,1)S(1)} %get-tuple-element.18.first_ref, bf16[4,64,512]{2,1,0:T(8,128)(2,1)S(1)} %get-tuple-element.17.second_ref, bf16[512,2048]{1,0:T(8,128)(2,1)S(1)} %bitcast.15, bf16[512,2048]{1,0:T(8,128)(2,1)} %collective-permute-done.far_hbm), custom_call_target="tpu_custom_call" | custom-call | flops 536870912 | bytes 6291456 | tf_op jit(solution)/shard_map/score_own/pallas_call | solution.py:136
  87.5 0.0 collective-permute-done.5.refs_2_
  87.5 0.0 collective-permute-done.6.refs_3_
  87.5 1.3 %score_sides.1.sides_ref = bf16[4,2,2,32,512]{4,3,2,1,0:T(8,128)(2,1)S(1)} custom-call(bf16[4,64,512]{2,1,0:T(8,128)(2,1)S(1)} %collective-permute-done.1.refs_0_, bf16[4,64,512]{2,1,0:T(8,128)(2,1)S(1)} %collective-permute-done.3.refs_1_, bf16[4,64,512]{2,1,0:T(8,128)(2,1)S(1)} %collective-permute-done.5.refs_2_, ...), custom_call_target="tpu_custom_call" | custom-call | flops 1073741824 | bytes 6291456 | tf_op jit(solution)/shard_map/score_sides/pallas_call | solution.py:147
  88.8 1.0 collective-permute-done.4.second_ref
  89.8 0.8 collective-permute-done.2.first_ref
  90.5 1.5 %score_last.1 = bf16[4,2,2,2,32,512]{5,4,3,2,1,0:T(8,128)(2,1)S(1)} custom-call(bf16[4,64,512]{2,1,0:T(8,128)(2,1)S(1)} %collective-permute-done.2.first_ref, bf16[4,64,512]{2,1,0:T(8,128)(2,1)S(1)} %collective-permute-done.4.second_ref, bf16[512,2048]{1,0:T(8,128)(2,1)S(1)} %bitcast.17, bf16[512,2048]{1,0:T(8,128)(2,1)S(1)} %get-tuple-element.13.refs_5_.far_ref, ...), custom_call_target="tpu_custom_call" | custom-call | flops 536870912 | bytes 6291456 | tf_op jit(solution)/shard_map/score_last/pallas_call | solution.py:153
  92.0 26.0 %all_to_all.10 = bf16[16,2,32,512]{3,2,1,0:T(8,128)(2,1)S(1)} all-to-all(bf16[16,2,32,512]{3,2,1,0:T(8,128)(2,1)S(1)} %bitcast.19), channel_id=1, replica_groups=mesh['z1'=2,'z0'=2,'y'=4,'x'=4,'zh'=4,'c'=2] {'y','c','z0'}, dimensions={0} | all-to-all | bytes 2097152 | tf_op jit(solution)/shard_map/all_to_all | solution.py:159
  118.0 0.1 sum_layers.1
  118.2 3.4 %collective-permute-start.7 = (bf16[2,32,512]{2,1,0:T(8,128)(2,1)S(1)}, bf16[2,32,512]{2,1,0:T(8,128)(2,1)S(1)}, u32[]{:S(2)}, u32[]{:S(2)}) collective-permute-start(bf16[2,32,512]{2,1,0:T(8,128)(2,1)S(1)} %get-tuple-element.16), channel_id=1, source_target_pairs={{0,256},{256,0},{1,257},{257,1},{2,258},{258,2},{3,259},{259,3},{4... | collective-permute-start | bytes 196616 | tf_op jit(solution)/shard_map/ppermute | solution.py:169
  121.6 2.5 %collective-permute-done.7 = bf16[2,32,512]{2,1,0:T(8,128)(2,1)S(1)} collective-permute-done((bf16[2,32,512]{2,1,0:T(8,128)(2,1)S(1)}, bf16[2,32,512]{2,1,0:T(8,128)(2,1)S(1)}, u32[]{:S(2)}, u32[]{:S(2)}) %collective-permute-start.7) | collective-permute-done | bytes 65568 | tf_op jit(solution)/shard_map/ppermute | solution.py:169
  124.1 0.7 convert_add_fusion
  (1 shorter events, 0.0 us)
Async XLA Ops:
  0.0 67.9 %collective-permute-start = (bf16[512,2048]{1,0:T(8,128)(2,1)}, bf16[512,2048]{1,0:T(8,128)(2,1)}, u32[]{:S(2)}, u32[]{:S(2)}) collective-permute-start(bf16[512,2048]{1,0:T(8,128)(2,1)} %bitcast.14), channel_id=1, source_target_pairs={{0,1},{1,0},{2,3},{3,2},{4,5},{5,4},{6,7},{7,6},{8,9},{9,8},{10,11... | collective-permute-start | bytes 6291464 | tf_op jit(solution)/shard_map/ppermute | solution.py:110
  11.3 3.7 %copy-start.1 = (bf16[1,32,2048]{2,1,0:T(8,128)(2,1)S(1)}, bf16[1,32,2048]{2,1,0:T(8,128)(2,1)}, u32[]{:S(2)}) copy-start(bf16[1,32,2048]{2,1,0:T(8,128)(2,1)} %param.4) | copy-start | bytes 393220
  11.3 30.0 %all-to-all-start = ((bf16[8,64,2048]{2,1,0:T(8,128)(2,1)}), bf16[8,64,2048]{2,1,0:T(8,128)(2,1)S(1)}, u32[]{:S(2)}, u32[]{:S(2)}) async-start(bf16[8,64,2048]{2,1,0:T(8,128)(2,1)} %broadcast_in_dim.8), calls=%async_computation | async-start | bytes 4194304 | tf_op jit(solution)/shard_map/all_to_all | solution.py:108
  41.3 43.7 %copy-start = (bf16[1,512,2048]{2,1,0:T(8,128)(2,1)S(1)}, bf16[1,512,2048]{2,1,0:T(8,128)(2,1)}, u32[]{:S(2)}) copy-start(bf16[1,512,2048]{2,1,0:T(8,128)(2,1)} %param.3) | copy-start | bytes 6291460
  67.9 11.8 %collective-permute-start.3 = (bf16[4,64,512]{2,1,0:T(8,128)(2,1)S(1)}, bf16[4,64,512]{2,1,0:T(8,128)(2,1)S(1)}, u32[]{:S(2)}, u32[]{:S(2)}) collective-permute-start(bf16[4,64,512]{2,1,0:T(8,128)(2,1)S(1)} %get-tuple-element.17.second_ref), channel_id=1, source_target_pairs={{0,24},{8,0},{16,8},{24,16},{1,25},{9,1},{17,9},{25,17},{2,26},{10... | collective-permute-start | bytes 786440 | tf_op jit(solution)/shard_map/ppermute | solution.py:36
  70.4 11.8 %collective-permute-start.1 = (bf16[4,64,512]{2,1,0:T(8,128)(2,1)S(1)}, bf16[4,64,512]{2,1,0:T(8,128)(2,1)S(1)}, u32[]{:S(2)}, u32[]{:S(2)}) collective-permute-start(bf16[4,64,512]{2,1,0:T(8,128)(2,1)S(1)} %get-tuple-element.18.first_ref), channel_id=1, source_target_pairs={{0,8},{8,16},{16,24},{24,0},{1,9},{9,17},{17,25},{25,1},{2,10},{10... | collective-permute-start | bytes 786440 | tf_op jit(solution)/shard_map/ppermute | solution.py:36
  73.2 14.3 %collective-permute-start.5 = (bf16[4,64,512]{2,1,0:T(8,128)(2,1)S(1)}, bf16[4,64,512]{2,1,0:T(8,128)(2,1)S(1)}, u32[]{:S(2)}, u32[]{:S(2)}) collective-permute-start(bf16[4,64,512]{2,1,0:T(8,128)(2,1)S(1)} %get-tuple-element.17.second_ref), channel_id=1, source_target_pairs={{0,8},{8,16},{16,24},{24,0},{1,9},{9,17},{17,25},{25,1},{2,10},{10... | collective-permute-start | bytes 786440 | tf_op jit(solution)/shard_map/ppermute | solution.py:36
  75.2 12.3 %collective-permute-start.6 = (bf16[4,64,512]{2,1,0:T(8,128)(2,1)S(1)}, bf16[4,64,512]{2,1,0:T(8,128)(2,1)S(1)}, u32[]{:S(2)}, u32[]{:S(2)}) collective-permute-start(bf16[4,64,512]{2,1,0:T(8,128)(2,1)S(1)} %get-tuple-element.18.first_ref), channel_id=1, source_target_pairs={{0,24},{8,0},{16,8},{24,16},{1,25},{9,1},{17,9},{25,17},{2,26},{10... | collective-permute-start | bytes 786440 | tf_op jit(solution)/shard_map/ppermute | solution.py:36
  79.7 10.0 %collective-permute-start.4 = (bf16[4,64,512]{2,1,0:T(8,128)(2,1)S(1)}, bf16[4,64,512]{2,1,0:T(8,128)(2,1)S(1)}, u32[]{:S(2)}, u32[]{:S(2)}) collective-permute-start(bf16[4,64,512]{2,1,0:T(8,128)(2,1)S(1)} %collective-permute-done.3.refs_1_), channel_id=1, source_target_pairs={{0,24},{8,0},{16,8},{24,16},{1,25},{9,1},{17,9},{25,17},{2,26},{10... | collective-permute-start | bytes 786440 | tf_op jit(solution)/shard_map/ppermute | solution.py:36
  82.2 8.3 %collective-permute-start.2 = (bf16[4,64,512]{2,1,0:T(8,128)(2,1)S(1)}, bf16[4,64,512]{2,1,0:T(8,128)(2,1)S(1)}, u32[]{:S(2)}, u32[]{:S(2)}) collective-permute-start(bf16[4,64,512]{2,1,0:T(8,128)(2,1)S(1)} %collective-permute-done.1.refs_0_), channel_id=1, source_target_pairs={{0,8},{8,16},{16,24},{24,0},{1,9},{9,17},{17,25},{25,1},{2,10},{10... | collective-permute-start | bytes 786440 | tf_op jit(solution)/shard_map/ppermute | solution.py:36
  118.2 5.9 %collective-permute-start.7 = (bf16[2,32,512]{2,1,0:T(8,128)(2,1)S(1)}, bf16[2,32,512]{2,1,0:T(8,128)(2,1)S(1)}, u32[]{:S(2)}, u32[]{:S(2)}) collective-permute-start(bf16[2,32,512]{2,1,0:T(8,128)(2,1)S(1)} %get-tuple-element.16), channel_id=1, source_target_pairs={{0,256},{256,0},{1,257},{257,1},{2,258},{258,2},{3,259},{259,3},{4... | collective-permute-start | bytes 196616 | tf_op jit(solution)/shard_map/ppermute | solution.py:169

commit v9 on v8

--- a/solution.py
+++ b/solution.py
@@ -118,8 +118,8 @@
         ),
         name="condition",
     )(queries, plane)
+    conditioned, far = lax.optimization_barrier((conditioned, far))
     conditioned = lax.all_gather(conditioned.reshape(2, 2 * mine, -1), "zh", axis=1)
-    conditioned, far = lax.optimization_barrier((conditioned, far))
     first, second = conditioned[0], conditioned[1]
     behind_first, ahead_second = shift_x(first, 1), shift_x(second, -1)
     behind_second, ahead_first = shift_x(second, 1), shift_x(first, -1)

time: 126 us -> 126 us (level)
  no operation moved by 1% of the time
where the time goes in v9:
time: 126 us; the launch traced here: 125 us
  blocking collectives  78.1 us (62%)
  starting transfers between devices  32.9 us (26%)
  Pallas kernels  6.07 us (5%)
  waiting for transfers between devices  4.26 us (3%)
  local copies, waits for them, and re-layouts  2.57 us (2%)
    all_gather x1, blocking collectives, on_device(): queries = lax.all_gather(query, 'zh', axis=0, tiled=True)  26.2 us
    all_to_all x1, blocking collectives, on_device(): lax.all_to_all(part.reshape(16, 2, mine, rows), ('y', 'c', 'z0'), 0, 0)  26 us
    all_gather x1, blocking collectives, on_device(): lax.all_gather(conditioned.reshape(2, 2 * mine, -1), 'zh', axis=1)  25.9 us
    ppermute x6, starting transfers between devices, shift_x(): return lax.ppermute(block, 'x', [(i, (i + by) % 4) for i in range(4)])  17.1 us
    ppermute x1, starting transfers between devices, on_device(): far = lax.ppermute(train, 'c', SWAP)  8.78 us
    all_to_all x1, starting transfers between devices, on_device(): plane = lax.all_to_all(copies(fisher, 8), ('x', 'c'), 0, 0)  3.68 us
    ppermute x1, starting transfers between devices, on_device(): total = keep + lax.ppermute(send, 'z1', SWAP).astype(jnp.float32)  3.42 us
    broadcast_in_dim x1, local copies, waits for them, and re-layouts, copies(): return jnp.broadcast_to(block[None], (n,) + block.shape)  2.53 us
  transfers between devices with their start and end apart: 9, of which 4 were waited for; matrix products, arithmetic and copies ran while one was open for 2% of the time, Pallas kernels for 4%

profile of v9, /device:TPU:1, one launch (start us, length us, event | category | flops | bytes accessed | tf_op | source)
XLA Modules:
  0.0 124.7 jit_solution(3481921461814977081)
XLA Ops:
  0.0 8.8 %collective-permute-start = (bf16[512,2048]{1,0:T(8,128)(2,1)}, bf16[512,2048]{1,0:T(8,128)(2,1)}, u32[]{:S(2)}, u32[]{:S(2)}) collective-permute-start(bf16[512,2048]{1,0:T(8,128)(2,1)} %bitcast.14), channel_id=1, source_target_pairs={{0,1},{1,0},{2,3},{3,2},{4,5},{5,4},{6,7},{7,6},{8,9},{9,8},{10,11... | collective-permute-start | bytes 6291464 | tf_op jit(solution)/shard_map/ppermute | solution.py:110
  8.8 2.5 %broadcast_in_dim.8 = bf16[8,64,2048]{2,1,0:T(8,128)(2,1)} broadcast(bf16[64,2048]{1,0:T(8,128)(2,1)} %bitcast.23), dimensions={1,2} | broadcast | bytes 2359296 | tf_op jit(solution)/shard_map/broadcast_in_dim | solution.py:15
  11.3 0.0 copy-start.1
  11.3 3.7 %all-to-all-start = ((bf16[8,64,2048]{2,1,0:T(8,128)(2,1)}), bf16[8,64,2048]{2,1,0:T(8,128)(2,1)S(1)}, u32[]{:S(2)}, u32[]{:S(2)}) async-start(bf16[8,64,2048]{2,1,0:T(8,128)(2,1)} %broadcast_in_dim.8), calls=%async_computation | async-start | bytes 4194304 | tf_op jit(solution)/shard_map/all_to_all | solution.py:108
  15.0 0.0 copy-done.1
  15.0 26.2 %all-gather = bf16[1,128,2048]{2,1,0:T(8,128)(2,1)S(1)} all-gather(bf16[1,32,2048]{2,1,0:T(8,128)(2,1)S(1)} %copy-done.1), channel_id=2, replica_groups=mesh['z1'=2,'z0'=2,'y'=4,'x'=4,'zh'=4,'c'=2] {'zh'}, dimensions={1}, use_global_device_ids=true | all-gather | bytes 655360 | tf_op jit(solution)/shard_map/all_gather | solution.py:111
  41.3 0.1 all-to-all-done
  41.3 0.0 copy-start
  41.3 0.7 condition.1
  42.0 0.0 collective-permute-done.far_hbm
  42.0 25.9 %all_gather.7 = bf16[2,4,64,512]{3,2,1,0:T(8,128)(2,1)S(1)} all-gather(bf16[2,1,64,512]{3,2,1,0:T(8,128)(2,1)S(1)} %bitcast.22), channel_id=1, replica_groups=mesh['z1'=2,'z0'=2,'y'=4,'x'=4,'zh'=4,'c'=2] {'zh'}, dimensions={1}, use_global_device_ids=true | all-gather | bytes 655360 | tf_op jit(solution)/shard_map/all_gather | solution.py:122
  67.9 2.4 %collective-permute-start.3 = (bf16[4,64,512]{2,1,0:T(8,128)(2,1)S(1)}, bf16[4,64,512]{2,1,0:T(8,128)(2,1)S(1)}, u32[]{:S(2)}, u32[]{:S(2)}) collective-permute-start(bf16[4,64,512]{2,1,0:T(8,128)(2,1)S(1)} %get-tuple-element.17.second_ref), channel_id=1, source_target_pairs={{0,24},{8,0},{16,8},{24,16},{1,25},{9,1},{17,9},{25,17},{2,26},{10... | collective-permute-start | bytes 786440 | tf_op jit(solution)/shard_map/ppermute | solution.py:36
  70.4 2.9 %collective-permute-start.1 = (bf16[4,64,512]{2,1,0:T(8,128)(2,1)S(1)}, bf16[4,64,512]{2,1,0:T(8,128)(2,1)S(1)}, u32[]{:S(2)}, u32[]{:S(2)}) collective-permute-start(bf16[4,64,512]{2,1,0:T(8,128)(2,1)S(1)} %get-tuple-element.18.first_ref), channel_id=1, source_target_pairs={{0,8},{8,16},{16,24},{24,0},{1,9},{9,17},{17,25},{25,1},{2,10},{10... | collective-permute-start | bytes 786440 | tf_op jit(solution)/shard_map/ppermute | solution.py:36
  73.2 2.0 %collective-permute-start.5 = (bf16[4,64,512]{2,1,0:T(8,128)(2,1)S(1)}, bf16[4,64,512]{2,1,0:T(8,128)(2,1)S(1)}, u32[]{:S(2)}, u32[]{:S(2)}) collective-permute-start(bf16[4,64,512]{2,1,0:T(8,128)(2,1)S(1)} %get-tuple-element.17.second_ref), channel_id=1, source_target_pairs={{0,8},{8,16},{16,24},{24,0},{1,9},{9,17},{17,25},{25,1},{2,10},{10... | collective-permute-start | bytes 786440 | tf_op jit(solution)/shard_map/ppermute | solution.py:36
  75.2 4.5 %collective-permute-start.6 = (bf16[4,64,512]{2,1,0:T(8,128)(2,1)S(1)}, bf16[4,64,512]{2,1,0:T(8,128)(2,1)S(1)}, u32[]{:S(2)}, u32[]{:S(2)}) collective-permute-start(bf16[4,64,512]{2,1,0:T(8,128)(2,1)S(1)} %get-tuple-element.18.first_ref), channel_id=1, source_target_pairs={{0,24},{8,0},{16,8},{24,16},{1,25},{9,1},{17,9},{25,17},{2,26},{10... | collective-permute-start | bytes 786440 | tf_op jit(solution)/shard_map/ppermute | solution.py:36
  79.7 0.0 collective-permute-done.3.refs_1_
  79.8 2.4 %collective-permute-start.4 = (bf16[4,64,512]{2,1,0:T(8,128)(2,1)S(1)}, bf16[4,64,512]{2,1,0:T(8,128)(2,1)S(1)}, u32[]{:S(2)}, u32[]{:S(2)}) collective-permute-start(bf16[4,64,512]{2,1,0:T(8,128)(2,1)S(1)} %collective-permute-done.3.refs_1_), channel_id=1, source_target_pairs={{0,24},{8,0},{16,8},{24,16},{1,25},{9,1},{17,9},{25,17},{2,26},{10... | collective-permute-start | bytes 786440 | tf_op jit(solution)/shard_map/ppermute | solution.py:36
  82.2 0.0 collective-permute-done.1.refs_0_
  82.2 2.8 %collective-permute-start.2 = (bf16[4,64,512]{2,1,0:T(8,128)(2,1)S(1)}, bf16[4,64,512]{2,1,0:T(8,128)(2,1)S(1)}, u32[]{:S(2)}, u32[]{:S(2)}) collective-permute-start(bf16[4,64,512]{2,1,0:T(8,128)(2,1)S(1)} %collective-permute-done.1.refs_0_), channel_id=1, source_target_pairs={{0,8},{8,16},{16,24},{24,0},{1,9},{9,17},{17,25},{25,1},{2,10},{10... | collective-permute-start | bytes 786440 | tf_op jit(solution)/shard_map/ppermute | solution.py:36
  85.1 0.0 copy-done
  85.1 2.4 %score_own.1 = (bf16[2,2,2,32,512]{4,3,2,1,0:T(8,128)(2,1)S(1)}, bf16[512,2048]{1,0:T(8,128)(2,1)S(1)}) custom-call(bf16[4,64,512]{2,1,0:T(8,128)(2,1)S(1)} %get-tuple-element.18.first_ref, bf16[4,64,512]{2,1,0:T(8,128)(2,1)S(1)} %get-tuple-element.17.second_ref, bf16[512,2048]{1,0:T(8,128)(2,1)S(1)} %bitcast.15, bf16[512,2048]{1,0:T(8,128)(2,1)} %collective-permute-done.far_hbm), custom_call_target="tpu_custom_call" | custom-call | flops 536870912 | bytes 6291456 | tf_op jit(solution)/shard_map/score_own/pallas_call | solution.py:136
  87.5 0.0 collective-permute-done.5.refs_2_
  87.5 0.0 collective-permute-done.6.refs_3_
  87.5 1.3 %score_sides.1.sides_ref = bf16[4,2,2,32,512]{4,3,2,1,0:T(8,128)(2,1)S(1)} custom-call(bf16[4,64,512]{2,1,0:T(8,128)(2,1)S(1)} %collective-permute-done.1.refs_0_, bf16[4,64,512]{2,1,0:T(8,128)(2,1)S(1)} %collective-permute-done.3.refs_1_, bf16[4,64,512]{2,1,0:T(8,128)(2,1)S(1)} %collective-permute-done.5.refs_2_, ...), custom_call_target="tpu_custom_call" | custom-call | flops 1073741824 | bytes 6291456 | tf_op jit(solution)/shard_map/score_sides/pallas_call | solution.py:147
  88.8 1.0 collective-permute-done.4.second_ref
  89.8 0.8 collective-permute-done.2.first_ref
  90.5 1.5 %score_last.1 = bf16[4,2,2,2,32,512]{5,4,3,2,1,0:T(8,128)(2,1)S(1)} custom-call(bf16[4,64,512]{2,1,0:T(8,128)(2,1)S(1)} %collective-permute-done.2.first_ref, bf16[4,64,512]{2,1,0:T(8,128)(2,1)S(1)} %collective-permute-done.4.second_ref, bf16[512,2048]{1,0:T(8,128)(2,1)S(1)} %bitcast.17, bf16[512,2048]{1,0:T(8,128)(2,1)S(1)} %get-tuple-element.13.refs_5_.far_ref, ...), custom_call_target="tpu_custom_call" | custom-call | flops 536870912 | bytes 6291456 | tf_op jit(solution)/shard_map/score_last/pallas_call | solution.py:153
  92.1 26.0 %all_to_all.10 = bf16[16,2,32,512]{3,2,1,0:T(8,128)(2,1)S(1)} all-to-all(bf16[16,2,32,512]{3,2,1,0:T(8,128)(2,1)S(1)} %bitcast.19), channel_id=1, replica_groups=mesh['z1'=2,'z0'=2,'y'=4,'x'=4,'zh'=4,'c'=2] {'y','c','z0'}, dimensions={0} | all-to-all | bytes 2097152 | tf_op jit(solution)/shard_map/all_to_all | solution.py:159
  118.0 0.1 sum_layers.1
  118.2 3.4 %collective-permute-start.7 = (bf16[2,32,512]{2,1,0:T(8,128)(2,1)S(1)}, bf16[2,32,512]{2,1,0:T(8,128)(2,1)S(1)}, u32[]{:S(2)}, u32[]{:S(2)}) collective-permute-start(bf16[2,32,512]{2,1,0:T(8,128)(2,1)S(1)} %get-tuple-element.16), channel_id=1, source_target_pairs={{0,256},{256,0},{1,257},{257,1},{2,258},{258,2},{3,259},{259,3},{4... | collective-permute-start | bytes 196616 | tf_op jit(solution)/shard_map/ppermute | solution.py:169
  121.6 2.5 %collective-permute-done.7 = bf16[2,32,512]{2,1,0:T(8,128)(2,1)S(1)} collective-permute-done((bf16[2,32,512]{2,1,0:T(8,128)(2,1)S(1)}, bf16[2,32,512]{2,1,0:T(8,128)(2,1)S(1)}, u32[]{:S(2)}, u32[]{:S(2)}) %collective-permute-start.7) | collective-permute-done | bytes 65568 | tf_op jit(solution)/shard_map/ppermute | solution.py:169
  124.1 0.7 convert_add_fusion
  (1 shorter events, 0.0 us)
Async XLA Ops:
  0.0 42.0 %collective-permute-start = (bf16[512,2048]{1,0:T(8,128)(2,1)}, bf16[512,2048]{1,0:T(8,128)(2,1)}, u32[]{:S(2)}, u32[]{:S(2)}) collective-permute-start(bf16[512,2048]{1,0:T(8,128)(2,1)} %bitcast.14), channel_id=1, source_target_pairs={{0,1},{1,0},{2,3},{3,2},{4,5},{5,4},{6,7},{7,6},{8,9},{9,8},{10,11... | collective-permute-start | bytes 6291464 | tf_op jit(solution)/shard_map/ppermute | solution.py:110
  11.3 3.7 %copy-start.1 = (bf16[1,32,2048]{2,1,0:T(8,128)(2,1)S(1)}, bf16[1,32,2048]{2,1,0:T(8,128)(2,1)}, u32[]{:S(2)}) copy-start(bf16[1,32,2048]{2,1,0:T(8,128)(2,1)} %param.4) | copy-start | bytes 393220
  11.3 30.0 %all-to-all-start = ((bf16[8,64,2048]{2,1,0:T(8,128)(2,1)}), bf16[8,64,2048]{2,1,0:T(8,128)(2,1)S(1)}, u32[]{:S(2)}, u32[]{:S(2)}) async-start(bf16[8,64,2048]{2,1,0:T(8,128)(2,1)} %broadcast_in_dim.8), calls=%async_computation | async-start | bytes 4194304 | tf_op jit(solution)/shard_map/all_to_all | solution.py:108
  41.3 43.7 %copy-start = (bf16[1,512,2048]{2,1,0:T(8,128)(2,1)S(1)}, bf16[1,512,2048]{2,1,0:T(8,128)(2,1)}, u32[]{:S(2)}) copy-start(bf16[1,512,2048]{2,1,0:T(8,128)(2,1)} %param.3) | copy-start | bytes 6291460
  67.9 11.8 %collective-permute-start.3 = (bf16[4,64,512]{2,1,0:T(8,128)(2,1)S(1)}, bf16[4,64,512]{2,1,0:T(8,128)(2,1)S(1)}, u32[]{:S(2)}, u32[]{:S(2)}) collective-permute-start(bf16[4,64,512]{2,1,0:T(8,128)(2,1)S(1)} %get-tuple-element.17.second_ref), channel_id=1, source_target_pairs={{0,24},{8,0},{16,8},{24,16},{1,25},{9,1},{17,9},{25,17},{2,26},{10... | collective-permute-start | bytes 786440 | tf_op jit(solution)/shard_map/ppermute | solution.py:36
  70.4 11.8 %collective-permute-start.1 = (bf16[4,64,512]{2,1,0:T(8,128)(2,1)S(1)}, bf16[4,64,512]{2,1,0:T(8,128)(2,1)S(1)}, u32[]{:S(2)}, u32[]{:S(2)}) collective-permute-start(bf16[4,64,512]{2,1,0:T(8,128)(2,1)S(1)} %get-tuple-element.18.first_ref), channel_id=1, source_target_pairs={{0,8},{8,16},{16,24},{24,0},{1,9},{9,17},{17,25},{25,1},{2,10},{10... | collective-permute-start | bytes 786440 | tf_op jit(solution)/shard_map/ppermute | solution.py:36
  73.2 14.3 %collective-permute-start.5 = (bf16[4,64,512]{2,1,0:T(8,128)(2,1)S(1)}, bf16[4,64,512]{2,1,0:T(8,128)(2,1)S(1)}, u32[]{:S(2)}, u32[]{:S(2)}) collective-permute-start(bf16[4,64,512]{2,1,0:T(8,128)(2,1)S(1)} %get-tuple-element.17.second_ref), channel_id=1, source_target_pairs={{0,8},{8,16},{16,24},{24,0},{1,9},{9,17},{17,25},{25,1},{2,10},{10... | collective-permute-start | bytes 786440 | tf_op jit(solution)/shard_map/ppermute | solution.py:36
  75.2 12.3 %collective-permute-start.6 = (bf16[4,64,512]{2,1,0:T(8,128)(2,1)S(1)}, bf16[4,64,512]{2,1,0:T(8,128)(2,1)S(1)}, u32[]{:S(2)}, u32[]{:S(2)}) collective-permute-start(bf16[4,64,512]{2,1,0:T(8,128)(2,1)S(1)} %get-tuple-element.18.first_ref), channel_id=1, source_target_pairs={{0,24},{8,0},{16,8},{24,16},{1,25},{9,1},{17,9},{25,17},{2,26},{10... | collective-permute-start | bytes 786440 | tf_op jit(solution)/shard_map/ppermute | solution.py:36
  79.8 10.0 %collective-permute-start.4 = (bf16[4,64,512]{2,1,0:T(8,128)(2,1)S(1)}, bf16[4,64,512]{2,1,0:T(8,128)(2,1)S(1)}, u32[]{:S(2)}, u32[]{:S(2)}) collective-permute-start(bf16[4,64,512]{2,1,0:T(8,128)(2,1)S(1)} %collective-permute-done.3.refs_1_), channel_id=1, source_target_pairs={{0,24},{8,0},{16,8},{24,16},{1,25},{9,1},{17,9},{25,17},{2,26},{10... | collective-permute-start | bytes 786440 | tf_op jit(solution)/shard_map/ppermute | solution.py:36
  82.2 8.3 %collective-permute-start.2 = (bf16[4,64,512]{2,1,0:T(8,128)(2,1)S(1)}, bf16[4,64,512]{2,1,0:T(8,128)(2,1)S(1)}, u32[]{:S(2)}, u32[]{:S(2)}) collective-permute-start(bf16[4,64,512]{2,1,0:T(8,128)(2,1)S(1)} %collective-permute-done.1.refs_0_), channel_id=1, source_target_pairs={{0,8},{8,16},{16,24},{24,0},{1,9},{9,17},{17,25},{25,1},{2,10},{10... | collective-permute-start | bytes 786440 | tf_op jit(solution)/shard_map/ppermute | solution.py:36
  118.2 5.9 %collective-permute-start.7 = (bf16[2,32,512]{2,1,0:T(8,128)(2,1)S(1)}, bf16[2,32,512]{2,1,0:T(8,128)(2,1)S(1)}, u32[]{:S(2)}, u32[]{:S(2)}) collective-permute-start(bf16[2,32,512]{2,1,0:T(8,128)(2,1)S(1)} %get-tuple-element.16), channel_id=1, source_target_pairs={{0,256},{256,0},{1,257},{257,1},{2,258},{258,2},{3,259},{259,3},{4... | collective-permute-start | bytes 196616 | tf_op jit(solution)/shard_map/ppermute | solution.py:169
